TPU v7x, 128 devices: a whole 4x4x4 slice. The times are simulated.
128 devices in a mesh: seq: 64 (over z, x_hi, y, core), head: 2 (over x_lo).
Axes of the slice: x: 4 (x_hi: 2, x_lo: 2; x = x_hi * 2 + x_lo), y: 4, z: 4, core: 2. Of those that a mesh axis runs over, the one named last changes fastest.
Arguments:
- tokens: bfloat16 [24576, 1536], P(('seq', 'head')), may hold values from -6 to 6
- cotangent: bfloat16 [24576, 1536], P(('seq', 'head')), may hold values from -24 to 24
- w_query: bfloat16 [1536, 1536], P(('seq', 'head')), may hold values from -0.3125 to 0.3125
- w_key: bfloat16 [1536, 128], P(('seq', 'head')), may hold values from -0.15625 to 0.15625
- w_value: bfloat16 [1536, 128], P(('seq', 'head')), may hold values from -0.15625 to 0.15625
- w_out: bfloat16 [1536, 1536], P('head', 'seq'), may hold values from -0.625 to 0.625
- w_gate: bfloat16 [1536, 4608], P('seq', 'head'), may hold values from -0.15625 to 0.15625
- w_up: bfloat16 [1536, 4608], P('seq', 'head'), may hold values from -0.15625 to 0.15625
- w_down: bfloat16 [4608, 1536], P('head', 'seq'), may hold values from -0.09375 to 0.09375
- gain_attn: bfloat16 [1536], P(('seq', 'head')), may hold values from 0.5 to 1.5
- gain_mlp: bfloat16 [1536], P(('seq', 'head')), may hold values from 0.5 to 1.5
Outputs:
- block_out: bfloat16 [24576, 1536], P(('seq', 'head'))
- input_grad: bfloat16 [24576, 1536], P(('seq', 'head'))
- grad_w_query: float32 [1536, 1536], P(('seq', 'head'))
- grad_w_key: float32 [1536, 128], P(('seq', 'head'))
- grad_w_value: float32 [1536, 128], P(('seq', 'head'))
- grad_w_out: float32 [1536, 1536], P('head', 'seq')
- grad_w_gate: float32 [1536, 4608], P('seq', 'head')
- grad_w_up: float32 [1536, 4608], P('seq', 'head')
- grad_w_down: float32 [4608, 1536], P('head', 'seq')
- grad_gain_attn: float32 [1536], P(('seq', 'head'))
- grad_gain_mlp: float32 [1536], P(('seq', 'head'))
All inputs are finite; a program needn't handle non-finite values.
Results may differ from a plain program's by a relative error of at most 0.02.
Values may be sent and summed in bfloat16 or wider, within the bound.
No kernel may reach another device: no remote copies, remote signals or barrier semaphores. Data moves between devices by JAX's collectives and lax.ppermute only.
A program may use at most 256 MiB of HBM per device.

v0:
```python
import jax
import jax.numpy as jnp
from jax import lax
from jax.sharding import PartitionSpec as P

WINDOW = 1024


EPSILON = 1e-06


def from_behind(block, axis, distance):
    devices = range(lax.axis_size(axis))
    route = [(i - distance, i) for i in devices if i - distance in devices]
    return lax.ppermute(block, axis, route)


def norm_rows(values_in, gain_vec):
    inverse = lax.rsqrt(jnp.mean(values_in * values_in, axis=-1, keepdims=True) + EPSILON)
    normed = values_in * inverse
    return (normed * gain_vec, normed, inverse)


def norm_back(grad_out, normed, inverse, gain_vec):
    scaled = grad_out * gain_vec
    return inverse * (scaled - normed * jnp.mean(scaled * normed, axis=-1, keepdims=True))


def geglu(gate, upward):
    return jax.nn.gelu(gate, approximate=True) * upward


def shards(
    tokens, cotangent, w_query, w_key, w_value, w_out, w_gate, w_up, w_down, gain_attn, gain_mlp
):
    local_rows = tokens.shape[0]
    width = tokens.shape[1]
    head_dim = w_key.shape[1]
    groups = lax.axis_size("head")
    shard_rows = groups * local_rows
    query_full, key_full, value_full, gain_first, gain_second = (
        lax.all_gather(w_query, ("seq", "head"), axis=0, tiled=True),
        lax.all_gather(w_key, ("seq", "head"), axis=0, tiled=True),
        lax.all_gather(w_value, ("seq", "head"), axis=0, tiled=True),
        lax.all_gather(gain_attn, ("seq", "head"), axis=0, tiled=True),
        lax.all_gather(gain_mlp, ("seq", "head"), axis=0, tiled=True),
    )
    out_rows, gate_cols, up_cols, down_rows = (
        lax.all_gather(w_out, "seq", axis=1, tiled=True),
        lax.all_gather(w_gate, "seq", axis=0, tiled=True),
        lax.all_gather(w_up, "seq", axis=0, tiled=True),
        lax.all_gather(w_down, "seq", axis=1, tiled=True),
    )
    first_gain = gain_first.astype(jnp.float32)
    second_gain = gain_second.astype(jnp.float32)
    key_value_w = jnp.concatenate([key_full, value_full], axis=1)
    inputs_float = tokens.astype(jnp.float32)
    first_scaled, first_normed, first_inverse = norm_rows(inputs_float, first_gain)
    first_low = first_scaled.astype(jnp.bfloat16)
    query_local = jnp.dot(first_low, query_full, preferred_element_type=jnp.float32).astype(
        jnp.bfloat16
    )
    keyval_local = jnp.dot(first_low, key_value_w, preferred_element_type=jnp.float32).astype(
        jnp.bfloat16
    )
    group_width = query_local.shape[1] // groups
    heads_group = group_width // head_dim
    query_split = query_local.reshape(local_rows, groups, group_width)
    keyval_split = jnp.broadcast_to(keyval_local[:, None, :], (local_rows, groups, 2 * head_dim))
    tokens_split = jnp.broadcast_to(tokens[:, None, :], (local_rows, groups, width))
    query_recv, keyval_recv, tokens_recv = (
        lax.all_to_all(query_split, "head", split_axis=1, concat_axis=0, tiled=True),
        lax.all_to_all(keyval_split, "head", split_axis=1, concat_axis=0, tiled=True),
        lax.all_to_all(tokens_split, "head", split_axis=1, concat_axis=0, tiled=True),
    )
    queries = query_recv.reshape(shard_rows, heads_group, head_dim)
    keyval_own = keyval_recv.reshape(shard_rows, 2 * head_dim)
    pair_inputs = tokens_recv.reshape(shard_rows, width).astype(jnp.float32)
    reach_count = -(-WINDOW // shard_rows)
    earlier = []
    carried = keyval_own
    for offset_step in range(1, reach_count + 1):
        source_block, hop_size = (carried, 1)
        carried = from_behind(source_block, "seq", hop_size)
        earlier.append(carried)
    key_table = jnp.concatenate(earlier[::-1] + [keyval_own], axis=0)
    key_part = key_table[:, :head_dim]
    value_part = key_table[:, head_dim:]
    seq_index = lax.axis_index("seq")
    query_pos = seq_index * shard_rows + jnp.arange(shard_rows, dtype=jnp.int32)
    key_pos = (seq_index - reach_count) * shard_rows + jnp.arange(
        key_table.shape[0], dtype=jnp.int32
    )
    distance = query_pos[:, None] - key_pos[None, :]
    allowed = (distance >= 0) & (distance < WINDOW) & (key_pos[None, :] >= 0)
    scale_factor = head_dim ** (-0.5)

    def score_table():
        raw_scores = (
            jnp.einsum("qhd,kd->hqk", queries, key_part, preferred_element_type=jnp.float32)
            * scale_factor
        )
        return jnp.where(allowed[None], raw_scores, -1e30)

    masked = score_table()
    highest = jnp.max(masked, axis=-1, keepdims=True)
    exponent_table = jnp.where(allowed[None], jnp.exp(masked - highest), 0.0)
    totals = jnp.sum(exponent_table, axis=-1, keepdims=True)
    log_total = highest + jnp.log(totals)
    attn_low = (exponent_table / totals).astype(jnp.bfloat16)
    attended = (
        jnp.einsum("hqk,kd->qhd", attn_low, value_part, preferred_element_type=jnp.float32)
        .reshape(shard_rows, group_width)
        .astype(jnp.bfloat16)
    )
    partial_out = jnp.dot(attended, out_rows, preferred_element_type=jnp.float32)
    branch_sum = lax.psum(partial_out.astype(jnp.bfloat16), "head").astype(jnp.float32)
    middle = pair_inputs + branch_sum
    second_scaled, second_normed, second_inverse = norm_rows(middle, second_gain)
    second_low = second_scaled.astype(jnp.bfloat16)
    gate_val = jnp.dot(second_low, gate_cols, preferred_element_type=jnp.float32)
    up_val = jnp.dot(second_low, up_cols, preferred_element_type=jnp.float32)
    hidden_float, geglu_back = jax.vjp(geglu, gate_val, up_val)
    hidden_low = hidden_float.astype(jnp.bfloat16)
    mlp_part = jnp.dot(hidden_low, down_rows, preferred_element_type=jnp.float32)
    mlp_own = lax.psum_scatter(
        mlp_part.astype(jnp.bfloat16), "head", scatter_dimension=0, tiled=True
    ).astype(jnp.float32)
    head_index = lax.axis_index("head")
    middle_own = lax.dynamic_slice_in_dim(middle, head_index * local_rows, local_rows, 0)
    block_out = (middle_own + mlp_own).astype(jnp.bfloat16)
    grad_rows = lax.all_gather(cotangent, "head", axis=0, tiled=True)
    grad_hidden = jnp.einsum("td,fd->tf", grad_rows, down_rows, preferred_element_type=jnp.float32)
    grad_gate, grad_upward = geglu_back(grad_hidden)
    gate_low = grad_gate.astype(jnp.bfloat16)
    upward_low = grad_upward.astype(jnp.bfloat16)
    second_part = jnp.einsum(
        "tf,df->td", gate_low, gate_cols, preferred_element_type=jnp.float32
    ) + jnp.einsum("tf,df->td", upward_low, up_cols, preferred_element_type=jnp.float32)
    second_grad = lax.psum(second_part.astype(jnp.bfloat16), "head").astype(jnp.float32)
    middle_grad = grad_rows.astype(jnp.float32) + norm_back(
        second_grad, second_normed, second_inverse, second_gain
    )
    own_second = lax.dynamic_slice_in_dim(second_grad, head_index * local_rows, local_rows, 0)
    own_normed = lax.dynamic_slice_in_dim(second_normed, head_index * local_rows, local_rows, 0)
    gain_second_grad = jnp.sum(own_second * own_normed, axis=0)
    middle_low = middle_grad.astype(jnp.bfloat16)
    attended_grad = (
        jnp.einsum("td,qd->tq", middle_low, out_rows, preferred_element_type=jnp.float32)
        .astype(jnp.bfloat16)
        .reshape(shard_rows, heads_group, head_dim)
    )
    masked_again = score_table()
    probs_again = jnp.where(allowed[None], jnp.exp(masked_again - log_total), 0.0)
    probs_low = probs_again.astype(jnp.bfloat16)
    prob_grad = jnp.einsum(
        "qhd,kd->hqk", attended_grad, value_part, preferred_element_type=jnp.float32
    )
    delta_sum = jnp.sum(probs_again * prob_grad, axis=-1, keepdims=True)
    score_grad = (probs_again * (prob_grad - delta_sum)).astype(jnp.bfloat16)
    query_grad = (
        jnp.einsum("hqk,kd->qhd", score_grad, key_part, preferred_element_type=jnp.float32)
        * scale_factor
    )
    key_grad = (
        jnp.einsum("hqk,qhd->kd", score_grad, queries, preferred_element_type=jnp.float32)
        * scale_factor
    )
    value_grad = jnp.einsum(
        "hqk,qhd->kd", probs_low, attended_grad, preferred_element_type=jnp.float32
    )
    keyval_grad = jnp.concatenate([key_grad, value_grad], axis=1)
    pieces = [
        keyval_grad[
            (reach_count - lag_count) * shard_rows : (reach_count - lag_count + 1) * shard_rows
        ]
        for lag_count in range(reach_count + 1)
    ]
    gathered_back = pieces[reach_count]
    for back_step in range(reach_count):
        source_block, hop_size = (gathered_back, -1)
        moved_block = from_behind(source_block.astype(jnp.bfloat16), "seq", hop_size).astype(
            source_block.dtype
        )
        gathered_back = moved_block + pieces[reach_count - 1 - back_step]
    query_send = query_grad.reshape(shard_rows, 1, group_width)
    keyval_send = gathered_back.reshape(shard_rows, 1, 2 * head_dim)
    query_home, keyval_home = (
        lax.all_to_all(
            query_send.astype(jnp.bfloat16), "head", split_axis=0, concat_axis=1, tiled=True
        ).astype(query_send.dtype),
        lax.all_to_all(
            keyval_send.astype(jnp.bfloat16), "head", split_axis=0, concat_axis=1, tiled=True
        ).astype(keyval_send.dtype),
    )
    query_home_low = query_home.reshape(local_rows, groups * group_width).astype(jnp.bfloat16)
    keyval_home_low = jnp.sum(keyval_home, axis=1).astype(jnp.bfloat16)
    first_grad = jnp.einsum(
        "tc,dc->td", query_home_low, query_full, preferred_element_type=jnp.float32
    ) + jnp.einsum("tc,dc->td", keyval_home_low, key_value_w, preferred_element_type=jnp.float32)
    grad_query_w = jnp.einsum(
        "td,tc->dc", first_low, query_home_low, preferred_element_type=jnp.float32
    )
    grad_keyval_w = jnp.einsum(
        "td,tc->dc", first_low, keyval_home_low, preferred_element_type=jnp.float32
    )
    gain_first_grad = jnp.sum(first_grad * first_normed, axis=0)
    first_input = norm_back(first_grad, first_normed, first_inverse, first_gain)
    middle_own_grad = lax.dynamic_slice_in_dim(middle_grad, head_index * local_rows, local_rows, 0)
    input_grad = (middle_own_grad + first_input).astype(jnp.bfloat16)
    grad_query_own, grad_key_own, grad_value_own, gain_first_own, gain_second_own = (
        lax.psum_scatter(grad_query_w, ("seq", "head"), scatter_dimension=0, tiled=True),
        lax.psum_scatter(
            grad_keyval_w[:, :head_dim], ("seq", "head"), scatter_dimension=0, tiled=True
        ),
        lax.psum_scatter(
            grad_keyval_w[:, head_dim:], ("seq", "head"), scatter_dimension=0, tiled=True
        ),
        lax.psum_scatter(gain_first_grad, ("seq", "head"), scatter_dimension=0, tiled=True),
        lax.psum_scatter(gain_second_grad, ("seq", "head"), scatter_dimension=0, tiled=True),
    )
    grad_down = jnp.einsum("tf,td->fd", hidden_low, grad_rows, preferred_element_type=jnp.float32)
    grad_gate_w = jnp.einsum("td,tf->df", second_low, gate_low, preferred_element_type=jnp.float32)
    grad_up_w = jnp.einsum("td,tf->df", second_low, upward_low, preferred_element_type=jnp.float32)
    grad_out_w = jnp.einsum("tq,td->qd", attended, middle_low, preferred_element_type=jnp.float32)
    grad_out_own, grad_gate_own, grad_up_own, grad_down_own = (
        lax.psum_scatter(grad_out_w, "seq", scatter_dimension=1, tiled=True),
        lax.psum_scatter(grad_gate_w, "seq", scatter_dimension=0, tiled=True),
        lax.psum_scatter(grad_up_w, "seq", scatter_dimension=0, tiled=True),
        lax.psum_scatter(grad_down, "seq", scatter_dimension=1, tiled=True),
    )
    return (
        block_out,
        input_grad,
        grad_query_own,
        grad_key_own,
        grad_value_own,
        grad_out_own,
        grad_gate_own,
        grad_up_own,
        grad_down_own,
        gain_first_own,
        gain_second_own,
    )


def solution(mesh):
    in_specs = (
        P(("seq", "head"), None),
        P(("seq", "head"), None),
        P(("seq", "head"), None),
        P(("seq", "head"), None),
        P(("seq", "head"), None),
        P("head", "seq"),
        P("seq", "head"),
        P("seq", "head"),
        P("head", "seq"),
        P(("seq", "head")),
        P(("seq", "head")),
    )
    out_specs = (
        P(("seq", "head"), None),
        P(("seq", "head"), None),
        P(("seq", "head"), None),
        P(("seq", "head"), None),
        P(("seq", "head"), None),
        P("head", "seq"),
        P("seq", "head"),
        P("seq", "head"),
        P("head", "seq"),
        P(("seq", "head")),
        P(("seq", "head")),
    )
    return jax.shard_map(shards, mesh=mesh, in_specs=in_specs, out_specs=out_specs, check_vma=False)
```

profile of v0, /device:TPU:64, one launch (start us, length us, event | category | flops | bytes accessed | tf_op | source)
XLA Modules:
  0.0 2228.0 jit_solution(15120238600103802487)
XLA Ops:
  9.7 66.2 %all-reduce.11 = (bf16[1536]{0:T(1024)(128)(2,1)S(1)}, bf16[1536]{0:T(1024)(128)(2,1)S(1)}) all-reduce(bf16[1536]{0:T(1024)(128)(2,1)S(1)} %dynamic-update-slice, bf16[1536]{0:T(1024)(128)(2,1)S(1)} %dynamic-update-slice.1), channel_id=1, replica_groups=mesh['seq'=64,'head'=2] {'seq','head'}, use_global_device_ids=true, to_apply=%add | all-reduce | flops 3072 | bytes 12288
  75.9 275.6 %all-gather = bf16[128,12,128]{2,1,0:T(8,128)(2,1)S(1)} all-gather(bf16[1,12,128]{2,1,0:T(8,128)(2,1)} %bitcast.128), channel_id=1, replica_groups=mesh['seq'=64,'head'=2] {'seq','head'}, dimensions={0}, use_global_device_ids=true | all-gather | bytes 396288 | tf_op jit(solution)/shard_map/all_gather | solution.py:43
  351.6 275.2 %all-gather.1 = bf16[128,12,128]{2,1,0:T(8,128)(2,1)S(1)} all-gather(bf16[1,12,128]{2,1,0:T(8,128)(2,1)} %bitcast.129), channel_id=1, replica_groups=mesh['seq'=64,'head'=2] {'seq','head'}, dimensions={0}, use_global_device_ids=true | all-gather | bytes 396288 | tf_op jit(solution)/shard_map/all_gather | solution.py:44
  636.9 9.5 collective-permute-done
  648.4 9.5 collective-permute-done.1
  659.9 8.2 reshape.174
  704.9 71.1 %all-gather.10.cloned.1.call-done = bf16[768,1536]{0,1:T(8,128)(2,1)} async-done(((bf16[768,24]{0,1:T(8,128)(2,1)}), bf16[768,1536]{0,1:T(8,128)(2,1)}) %all-gather.10.cloned.1.call-update) | async-done | bytes 2359312 | tf_op jit(solution)/shard_map/all_gather | solution.py:49
  788.2 26.5 %all-to-all-done = bf16[192,2,1536]{2,0,1:T(8,128)(2,1)} async-done(((bf16[192,2,1536]{2,0,1:T(8,128)(2,1)}), bf16[192,2,1536]{2,0,1:T(8,128)(2,1)}, u32[]{:S(2)}, u32[]{:S(2)}) %all-to-all-start) | async-done | bytes 1179680 | tf_op jit(solution)/shard_map/all_to_all | solution.py:74
  816.2 23.9 %all-reduce.16.cloned.1.call-done = bf16[384,1536]{1,0:T(8,128)(2,1)} async-done(((bf16[384,1536]{1,0:T(8,128)(2,1)}), bf16[384,1536]{1,0:T(8,128)(2,1)}) %all-reduce.16.cloned.1.call-update) | async-done | bytes 1179664 | tf_op jit(solution)/shard_map/psum | solution.py:117
  844.6 78.4 %all-gather.14.cloned.1.call-done = bf16[1536,2304]{1,0:T(8,128)(2,1)} async-done(((bf16[24,2304]{1,0:T(8,128)(2,1)}), bf16[1536,2304]{1,0:T(8,128)(2,1)}) %all-gather.14.cloned.1.call-update) | async-done | bytes 7077904 | tf_op jit(solution)/shard_map/all_gather | solution.py:51
  923.0 8.1 fusion.67
  931.0 72.6 %all-gather.12.cloned.1.call-done = bf16[1536,2304]{1,0:T(8,128)(2,1)} async-done(((bf16[24,2304]{1,0:T(8,128)(2,1)}), bf16[1536,2304]{1,0:T(8,128)(2,1)}) %all-gather.12.cloned.1.call-update) | async-done | bytes 7077904 | tf_op jit(solution)/shard_map/all_gather | solution.py:50
  1003.6 8.0 fusion.66
  1011.6 17.7 all-gather.18.cloned.1.call-done
  1029.4 82.9 %all-gather.16.cloned.1.call-done = bf16[2304,1536]{0,1:T(8,128)(2,1)} async-done(((bf16[2304,24]{0,1:T(8,128)(2,1)}), bf16[2304,1536]{0,1:T(8,128)(2,1)}) %all-gather.16.cloned.1.call-update) | async-done | bytes 7077904 | tf_op jit(solution)/shard_map/all_gather | solution.py:52
  1112.3 10.2 multiply_convert_fusion
  1140.5 40.4 %all-reduce.18.cloned.1.call-done = bf16[384,1536]{1,0:T(8,128)(2,1)} async-done(((bf16[384,1536]{1,0:T(8,128)(2,1)}), bf16[384,1536]{1,0:T(8,128)(2,1)}) %all-reduce.18.cloned.1.call-update) | async-done | bytes 1179664 | tf_op jit(solution)/shard_map/psum | solution.py:140
  1188.7 10.6 fusion.72
  1199.4 10.8 fusion.71
  1210.4 10.8 fusion.70
  1228.4 14.8 fusion.3
  1243.2 7.5 fusion.5
  1266.3 8.3 collective-permute-start.4
  1322.3 365.9 %fusion.63 = (f32[16,1536]{1,0:T(8,128)}, f32[16,128]{1,0:T(8,128)}, f32[16,128]{1,0:T(8,128)}) fusion(f32[1536,1536]{1,0:T(8,128)} %fusion.59, f32[1536,128]{1,0:T(8,128)} %get-tuple-element.31, f32[1536,128]{1,0:T(8,128)} %get-tuple-element.30), kind=kCustom, calls=%all-reduce-scatter.3 | all-reduce-scatter fusion | flops 3670017 | bytes 11124736
  1688.9 35.2 %collective-permute-start.101 = (f32[12,128]{1,0:T(8,128)S(1)}, f32[12,128]{1,0:T(8,128)}, u32[]{:S(2)}, u32[]{:S(2)}) collective-permute-start(f32[12,128]{1,0:T(8,128)S(1)} %slice.45), channel_id=1, source_target_pairs={{0,32},{1,33},{2,34},{3,35},{4,36},{5,37},{6,38},{7,39},{8,40},{9,... | collective-permute-start | bytes 18440
  1808.7 16.2 collective-permute-start.100
  1898.5 15.8 collective-permute-start.75
  1946.9 8.1 collective-permute-done.35
  1996.7 71.8 %all-reduce.10 = (f32[1536]{0:T(1024)S(1)}, f32[1536]{0:T(1024)S(1)}) all-reduce(f32[1536]{0:T(1024)} %get-tuple-element.11, f32[1536]{0:T(1024)} %multiply_reduce_fusion.2), channel_id=10, replica_groups=mesh['seq'=64,'head'=2] {'seq','head'}, use_global_device_ids=true, to_apply=%region_19.20.clone | all-reduce | flops 3072 | bytes 24576
  2069.7 25.2 %concatenate.13 = f32[524,128]{1,0:T(8,128)S(1)} concatenate(f32[12,128]{1,0:T(8,128)} %collective-permute-done.69, f32[16,128]{1,0:T(8,128)} %collective-permute-done.68, f32[16,128]{1,0:T(8,128)} %collective-permute-done.67, f32[16,128]{1,0:T(8,128)} %collective-permute-done.66, f32[16,128]{1,0:T(8,128)} %collective-permute-done.65, f32[16,128]{1,0:T(8,128)} %collective-permute-done.64, ...), dimensions={0} | concatenate | bytes 536576
  2094.9 25.3 %concatenate.14 = f32[524,128]{1,0:T(8,128)S(1)} concatenate(f32[12,128]{1,0:T(8,128)} %collective-permute-done.101, f32[16,128]{1,0:T(8,128)} %collective-permute-done.100, f32[16,128]{1,0:T(8,128)} %collective-permute-done.99, f32[16,128]{1,0:T(8,128)} %collective-permute-done.98, f32[16,128]{1,0:T(8,128)} %collective-permute-done.97, f32[16,128]{1,0:T(8,128)} %collective-permute-done.96, ...), dimensions={0} | concatenate | bytes 536576
  2165.2 52.3 %concatenate.12 = f32[524,1536]{1,0:T(8,128)} concatenate(f32[12,1536]{1,0:T(8,128)} %collective-permute-done.37, f32[16,1536]{1,0:T(8,128)} %collective-permute-done.36, f32[16,1536]{1,0:T(8,128)} %copy-done.30, f32[16,1536]{1,0:T(8,128)} %copy-done.31, f32[16,1536]{1,0:T(8,128)} %copy-done.32, f32[16,1536]{1,0:T(8,128)} %copy-done.33, f32[16,1536]{1,0:T(8,128)} %copy-done.34, ...), dimensions={0} | concatenate | bytes 6438912
  (413 shorter events, 448.6 us)
Async XLA Ops:
  7.2 652.7 %all-gather.20.cloned.1.call-start = ((), (), s32[]{:S(2)}) async-start(), calls=%async_computation.22 | async-start | bytes 6340608 | tf_op jit(solution)/shard_map/all_gather | solution.py:42
  7.9 768.1 %all-gather.10.cloned.1.call-start = ((), (), s32[]{:S(2)}) async-start(), calls=%async_computation.10 | async-start | bytes 2396160 | tf_op jit(solution)/shard_map/all_gather | solution.py:49
  675.9 164.2 %all-reduce.16.cloned.1.call-start = ((), (), s32[]{:S(2)}) async-start(), calls=%async_computation.11 | async-start | bytes 2359296 | tf_op jit(solution)/shard_map/psum | solution.py:117
  779.8 143.1 %all-gather.14.cloned.1.call-start = ((), (), s32[]{:S(2)}) async-start(), calls=%async_computation.13 | async-start | bytes 7188480 | tf_op jit(solution)/shard_map/all_gather | solution.py:51
  780.4 223.2 %all-gather.12.cloned.1.call-start = ((), (), s32[]{:S(2)}) async-start(), calls=%async_computation.12 | async-start | bytes 7188480 | tf_op jit(solution)/shard_map/all_gather | solution.py:50
  781.0 248.4 %all-gather.18.cloned.1.call-start = ((), (), s32[]{:S(2)}) async-start(), calls=%async_computation.16 | async-start | bytes 1769472 | tf_op jit(solution)/shard_map/all_gather | solution.py:132
  781.6 330.7 %all-gather.16.cloned.1.call-start = ((), (), s32[]{:S(2)}) async-start(), calls=%async_computation.14 | async-start | bytes 7188480 | tf_op jit(solution)/shard_map/all_gather | solution.py:52
  783.4 31.2 %all-to-all-start = ((bf16[192,2,1536]{2,0,1:T(8,128)(2,1)}), bf16[192,2,1536]{2,0,1:T(8,128)(2,1)}, u32[]{:S(2)}, u32[]{:S(2)}) async-start(bf16[192,2,1536]{2,0,1:T(8,128)(2,1)} %broadcast_in_dim.30), calls=%async_computation | async-start | bytes 2359296 | tf_op jit(solution)/shard_map/all_to_all | solution.py:74
  787.9 393.0 %all-reduce.18.cloned.1.call-start = ((), (), s32[]{:S(2)}) async-start(), calls=%async_computation.17 | async-start | bytes 2359296 | tf_op jit(solution)/shard_map/psum | solution.py:140
  1132.5 1086.5 %reduce-scatter.12.cloned.1.call-start = ((), (), s32[]{:S(2)}) async-start(), calls=%async_computation.15 | async-start | bytes 1769472 | tf_op jit(solution)/shard_map/reduce_scatter | solution.py:126
  1140.4 1080.6 %reduce-scatter.14.cloned.1.call-start = ((), (), s32[]{:S(2)}) async-start(), calls=%async_computation.18 | async-start | bytes 4792320 | tf_op jit(solution)/shard_map/reduce_scatter | solution.py:227
  1188.6 1032.4 %reduce-scatter.20.cloned.1.call-start = ((), (), s32[]{:S(2)}) async-start(), calls=%async_computation.21 | async-start | bytes 14376960 | tf_op jit(solution)/shard_map/reduce_scatter | solution.py:230
  1199.3 1021.7 %reduce-scatter.18.cloned.1.call-start = ((), (), s32[]{:S(2)}) async-start(), calls=%async_computation.20 | async-start | bytes 14376960 | tf_op jit(solution)/shard_map/reduce_scatter | solution.py:229
  1210.2 1010.8 %reduce-scatter.16.cloned.1.call-start = ((), (), s32[]{:S(2)}) async-start(), calls=%async_computation.19 | async-start | bytes 14376960 | tf_op jit(solution)/shard_map/reduce_scatter | solution.py:228
  1688.9 50.0 %collective-permute-start.101 = (f32[12,128]{1,0:T(8,128)S(1)}, f32[12,128]{1,0:T(8,128)}, u32[]{:S(2)}, u32[]{:S(2)}) collective-permute-start(f32[12,128]{1,0:T(8,128)S(1)} %slice.45), channel_id=1, source_target_pairs={{0,32},{1,33},{2,34},{3,35},{4,36},{5,37},{6,38},{7,39},{8,40},{9,... | collective-permute-start | bytes 18440
  1799.3 25.7 %collective-permute-start.41 = (f32[16,128]{1,0:T(8,128)}, f32[16,128]{1,0:T(8,128)}, u32[]{:S(2)}, u32[]{:S(2)}) collective-permute-start(f32[16,128]{1,0:T(8,128)} %get-tuple-element.21), channel_id=1, source_target_pairs={{0,4},{1,5},{2,6},{3,7},{4,8},{5,9},{6,10},{7,11},{8,12},{9,13},{1... | collective-permute-start | bytes 24584
  1801.2 30.7 %collective-permute-start.40 = (f32[16,128]{1,0:T(8,128)}, f32[16,128]{1,0:T(8,128)}, u32[]{:S(2)}, u32[]{:S(2)}) collective-permute-start(f32[16,128]{1,0:T(8,128)} %get-tuple-element.21), channel_id=1, source_target_pairs={{0,3},{1,4},{2,5},{3,6},{4,7},{5,8},{6,9},{7,10},{8,11},{9,12},{10... | collective-permute-start | bytes 24584
  1804.5 29.9 %collective-permute-start.39 = (f32[16,128]{1,0:T(8,128)}, f32[16,128]{1,0:T(8,128)}, u32[]{:S(2)}, u32[]{:S(2)}) collective-permute-start(f32[16,128]{1,0:T(8,128)} %get-tuple-element.21), channel_id=1, source_target_pairs={{0,2},{1,3},{2,4},{3,5},{4,6},{5,7},{6,8},{7,9},{8,10},{9,11},{10,... | collective-permute-start | bytes 24584
  1806.4 30.2 %collective-permute-start.38 = (f32[16,128]{1,0:T(8,128)}, f32[16,128]{1,0:T(8,128)}, u32[]{:S(2)}, u32[]{:S(2)}) collective-permute-start(f32[16,128]{1,0:T(8,128)} %get-tuple-element.21), channel_id=1, source_target_pairs={{0,1},{1,2},{2,3},{3,4},{4,5},{5,6},{6,7},{7,8},{8,9},{9,10},{10,1... | collective-permute-start | bytes 24584
  1808.7 30.1 %collective-permute-start.100 = (f32[16,128]{1,0:T(8,128)}, f32[16,128]{1,0:T(8,128)}, u32[]{:S(2)}, u32[]{:S(2)}) collective-permute-start(f32[16,128]{1,0:T(8,128)} %get-tuple-element.22), channel_id=1, source_target_pairs={{0,31},{1,32},{2,33},{3,34},{4,35},{5,36},{6,37},{7,38},{8,39},{9,... | collective-permute-start | bytes 24584
  1832.0 108.9 %collective-permute-start.36 = (f32[16,1536]{1,0:T(8,128)}, f32[16,1536]{1,0:T(8,128)}, u32[]{:S(2)}, u32[]{:S(2)}) collective-permute-start(f32[16,1536]{1,0:T(8,128)} %get-tuple-element.20), channel_id=1, source_target_pairs={{0,31},{1,32},{2,33},{3,34},{4,35},{5,36},{6,37},{7,38},{8,39},{9,... | collective-permute-start | bytes 294920
  1861.5 77.5 %collective-permute-start.37 = (f32[12,1536]{1,0:T(8,128)}, f32[12,1536]{1,0:T(8,128)}, u32[]{:S(2)}, u32[]{:S(2)}) collective-permute-start(f32[12,1536]{1,0:T(8,128)} %slice.43), channel_id=1, source_target_pairs={{0,32},{1,33},{2,34},{3,35},{4,36},{5,37},{6,38},{7,39},{8,40},{9,... | collective-permute-start | bytes 221192
  1933.1 21.8 collective-permute-start.35
  1935.1 21.8 collective-permute-start.34
  1937.0 21.8 collective-permute-start.33
  1939.0 21.8 collective-permute-start.32
  1982.5 137.7 %collective-permute-start.20 = (f32[16,1536]{1,0:T(8,128)}, f32[16,1536]{1,0:T(8,128)}, u32[]{:S(2)}, u32[]{:S(2)}) collective-permute-start(f32[16,1536]{1,0:T(8,128)} %get-tuple-element.20), channel_id=1, source_target_pairs={{0,15},{1,16},{2,17},{3,18},{4,19},{5,20},{6,21},{7,22},{8,23},{9,... | collective-permute-start | bytes 294920
  1984.4 138.3 %collective-permute-start.19 = (f32[16,1536]{1,0:T(8,128)}, f32[16,1536]{1,0:T(8,128)}, u32[]{:S(2)}, u32[]{:S(2)}) collective-permute-start(f32[16,1536]{1,0:T(8,128)} %get-tuple-element.20), channel_id=1, source_target_pairs={{0,14},{1,15},{2,16},{3,17},{4,18},{5,19},{6,20},{7,21},{8,22},{9,... | collective-permute-start | bytes 294920
  1987.3 140.6 %collective-permute-start.18 = (f32[16,1536]{1,0:T(8,128)}, f32[16,1536]{1,0:T(8,128)}, u32[]{:S(2)}, u32[]{:S(2)}) collective-permute-start(f32[16,1536]{1,0:T(8,128)} %get-tuple-element.20), channel_id=1, source_target_pairs={{0,13},{1,14},{2,15},{3,16},{4,17},{5,18},{6,19},{7,20},{8,21},{9,... | collective-permute-start | bytes 294920
  1991.7 138.8 %collective-permute-start.17 = (f32[16,1536]{1,0:T(8,128)}, f32[16,1536]{1,0:T(8,128)}, u32[]{:S(2)}, u32[]{:S(2)}) collective-permute-start(f32[16,1536]{1,0:T(8,128)} %get-tuple-element.20), channel_id=1, source_target_pairs={{0,12},{1,13},{2,14},{3,15},{4,16},{5,17},{6,18},{7,19},{8,20},{9,... | collective-permute-start | bytes 294920
  1993.6 140.6 %collective-permute-start.16 = (f32[16,1536]{1,0:T(8,128)}, f32[16,1536]{1,0:T(8,128)}, u32[]{:S(2)}, u32[]{:S(2)}) collective-permute-start(f32[16,1536]{1,0:T(8,128)} %get-tuple-element.20), channel_id=1, source_target_pairs={{0,11},{1,12},{2,13},{3,14},{4,15},{5,16},{6,17},{7,18},{8,19},{9,... | collective-permute-start | bytes 294920
  2130.5 22.3 collective-permute-start.12
  (134 other events, 3639.2 us)
Sparse Core Ops, SparseCore 0:
  9.7 311.2 all-gather.19
  637.0 138.9 all-gather.9
  780.0 60.1 all-reduce.15
  843.7 79.2 all-gather.13
  926.5 77.0 all-gather.11
  1005.2 24.1 all-gather.17
  1033.0 79.2 all-gather.15
  1132.6 48.2 all-reduce.17
  1183.3 25.2 reduce-scatter.11
  1215.3 154.6 reduce-scatter.13
  1377.5 220.0 reduce-scatter.19
  1605.0 188.6 reduce-scatter.17
  1801.2 206.1 reduce-scatter.15
where the time goes:
time: 2240 us; the launch traced here: 2230 us
  blocking collectives  1060 us (47%)
  waiting for transfers between devices  475 us (21%)
  starting transfers between devices  353 us (16%)
  local copies, waits for them, and re-layouts  143 us (6%)
  matrix products  138 us (6%)
  other arithmetic  40 us (2%)
    unnamed x3, blocking collectives  504 us
    unnamed x96, starting transfers between devices  313 us
    all_gather x1, blocking collectives, shards(): lax.all_gather(w_key, ('seq', 'head'), axis=0, tiled=True)  276 us
    all_gather x1, blocking collectives, shards(): lax.all_gather(w_value, ('seq', 'head'), axis=0, tiled=True)  275 us
    unnamed x122, local copies, waits for them, and re-layouts  136 us
    all_gather x1, waiting for transfers between devices, shards(): lax.all_gather(w_down, 'seq', axis=1, tiled=True)  82.9 us
    all_gather x1, waiting for transfers between devices, shards(): lax.all_gather(w_up, 'seq', axis=0, tiled=True)  78.4 us
    all_gather x1, waiting for transfers between devices, shards(): lax.all_gather(w_gate, 'seq', axis=0, tiled=True)  72.6 us
  transfers between devices with their start and end apart: 119, of which 23 were waited for; matrix products, arithmetic and copies ran while one was open for 30% of the time, Pallas kernels for 0%

commit v1 on v0

v1 whole, which is shorter than its diff:
```python
import functools
import jax
import jax.numpy as jnp
from jax import lax
from jax.experimental import pallas as pl
from jax.experimental.pallas import tpu as pltpu
from jax.sharding import Mesh
from jax.sharding import PartitionSpec as P

WINDOW = 1024
EPSILON = 1e-06
AXES = ("z", "xh", "y", "core", "head")
SIZES = (4, 2, 4, 2, 2)
CHIPS_X = ("xh", "head")
PLANE = ("z", "y")
ROW = 192
KEYS = 1216
HEADS = 12
HD = 128
BF = jnp.bfloat16
F32 = jnp.float32
NEG = -1e30
SCALE = HD ** (-0.5)
LOG2E = 1.4426950408889634
VMEM_BYTES = 56 * 1024 * 1024

NN = (((1,), (0,)), ((), ()))
NT = (((1,), (1,)), ((), ()))
TN = (((0,), (0,)), ((), ()))


def dot(a, b, dims=NN):
    return lax.dot_general(a, b, dims, preferred_element_type=F32)


def two_heads(pair):
    return jnp.concatenate([pair[:, :HD], pair[:, HD:]], axis=0)


def attend_kernel(block_ref, q_ref, kv_ref, out_ref, probs_ref, bias):
    @pl.when(pl.program_id(0) == 0)
    def _():
        key = lax.broadcasted_iota(jnp.int32, (KEYS, ROW), 0)
        query = lax.broadcasted_iota(jnp.int32, (KEYS, ROW), 1)
        first = WINDOW - ROW * block_ref[0]
        inside = (key > query) & (key <= query + WINDOW) & (key >= first)
        one = jnp.where(inside, 0.0, NEG)
        bias[:, :] = jnp.concatenate([one, one], axis=1)

    queries = two_heads(q_ref[...])
    scores = dot(kv_ref[:, :HD], queries, NT) + bias[...]
    highest = jnp.max(scores, axis=0, keepdims=True)
    powers = jnp.exp2((scores - highest) * (SCALE * LOG2E))
    total = jnp.sum(powers, axis=0, keepdims=True)
    probs = (powers * (1.0 / total)).astype(BF)
    probs_ref[0] = probs
    mixed = dot(kv_ref[:, HD:], probs, TN).T.astype(BF)
    out_ref[...] = jnp.concatenate([mixed[:ROW], mixed[ROW:]], axis=1)


def attend(block, queries, keyval):
    return pl.pallas_call(
        attend_kernel,
        grid_spec=pltpu.PrefetchScalarGridSpec(
            num_scalar_prefetch=1,
            grid=(HEADS // 2,),
            in_specs=[
                pl.BlockSpec((ROW, 2 * HD), lambda h, b: (0, h)),
                pl.BlockSpec((KEYS, 2 * HD), lambda h, b: (0, 0)),
            ],
            out_specs=[
                pl.BlockSpec((ROW, 2 * HD), lambda h, b: (0, h)),
                pl.BlockSpec((1, KEYS, 2 * ROW), lambda h, b: (h, 0, 0)),
            ],
            scratch_shapes=[pltpu.VMEM((KEYS, 2 * ROW), F32)],
        ),
        out_shape=[
            jax.ShapeDtypeStruct((ROW, HEADS * HD), BF),
            jax.ShapeDtypeStruct((HEADS // 2, KEYS, 2 * ROW), BF),
        ],
        compiler_params=pltpu.CompilerParams(vmem_limit_bytes=VMEM_BYTES),
        cost_estimate=pl.CostEstimate(
            flops=4 * HEADS * ROW * KEYS * HD,
            bytes_accessed=8 * 1024 * 1024,
            transcendentals=HEADS * ROW * KEYS,
        ),
        name="attend",
    )(block, queries, keyval)


def attend_back_kernel(q_ref, kv_ref, out_ref, grad_ref, probs_ref, dq_ref, dkv_ref, dk, dv):
    step = pl.program_id(0)

    @pl.when(step == 0)
    def _():
        dk[...] = jnp.zeros_like(dk)
        dv[...] = jnp.zeros_like(dv)

    queries = two_heads(q_ref[...])
    grads = two_heads(grad_ref[...])
    outs = two_heads(out_ref[...])
    probs = probs_ref[0]
    delta = jnp.sum((grads.astype(F32) * outs.astype(F32)).T, axis=0, keepdims=True)
    dprobs = dot(kv_ref[:, HD:], grads, NT)
    dscores = (probs.astype(F32) * (dprobs - delta)).astype(BF)
    dqueries = (dot(kv_ref[:, :HD], dscores, TN).T * SCALE).astype(BF)
    dq_ref[...] = jnp.concatenate([dqueries[:ROW], dqueries[ROW:]], axis=1)
    dk[...] += dot(dscores, queries)
    dv[...] += dot(probs, grads)

    @pl.when(step == HEADS // 2 - 1)
    def _():
        dkv_ref[:, :HD] = (dk[...] * SCALE).astype(BF)
        dkv_ref[:, HD:] = dv[...].astype(BF)


def attend_back(queries, keyval, attended, grads, probs):
    pair = pl.BlockSpec((ROW, 2 * HD), lambda h: (0, h))
    table = pl.BlockSpec((KEYS, 2 * HD), lambda h: (0, 0))
    return pl.pallas_call(
        attend_back_kernel,
        grid=(HEADS // 2,),
        in_specs=[pair, table, pair, pair, pl.BlockSpec((1, KEYS, 2 * ROW), lambda h: (h, 0, 0))],
        out_specs=[pair, table],
        scratch_shapes=[pltpu.VMEM((KEYS, HD), F32), pltpu.VMEM((KEYS, HD), F32)],
        out_shape=[
            jax.ShapeDtypeStruct((ROW, HEADS * HD), BF),
            jax.ShapeDtypeStruct((KEYS, 2 * HD), BF),
        ],
        compiler_params=pltpu.CompilerParams(vmem_limit_bytes=VMEM_BYTES),
        cost_estimate=pl.CostEstimate(
            flops=8 * HEADS * ROW * KEYS * HD,
            bytes_accessed=9 * 1024 * 1024,
            transcendentals=0,
        ),
        name="attend_back",
    )(queries, keyval, attended, grads, probs)


def shift_all(block, distance):
    count = 128
    route = [(i, i + distance) for i in range(count) if 0 <= i + distance < count]
    return lax.ppermute(block, AXES, route)


def shift_x(block, distance):
    return lax.ppermute(block, CHIPS_X, [(i, (i + distance) % 4) for i in range(4)])


def swap_core(block):
    return lax.ppermute(block, "core", [(0, 1), (1, 0)])


def mixed_order(rows):
    count = rows.shape[0]
    return rows.reshape(count, 4, 2, 192).transpose(0, 2, 1, 3).reshape(count, 1536)


def true_order(rows):
    count = rows.shape[0]
    return rows.reshape(count, 2, 4, 192).transpose(0, 2, 1, 3).reshape(count, 1536)


def shards(tokens, cotangent, w_query, w_key, w_value, w_out, w_gate, w_up, w_down, gain_attn, gain_mlp):
    core = lax.axis_index("core")
    xh = lax.axis_index("xh")
    block = lax.axis_index(AXES)

    def halves(full, axis):
        size = full.shape[axis] // 2
        return (
            lax.dynamic_slice_in_dim(full, core * size, size, axis),
            lax.dynamic_slice_in_dim(full, (1 - core) * size, size, axis),
        )

    def joined(mine, other, axis):
        return jnp.concatenate(
            [jnp.where(core == 0, mine, other), jnp.where(core == 0, other, mine)], axis=axis
        )

    def spread(piece):
        mine = lax.all_gather(piece, PLANE, axis=0, tiled=True)
        return mine, swap_core(mine)

    gains = jnp.pad(jnp.stack([gain_attn, gain_mlp], axis=1), ((0, 0), (0, 126)))
    own_qkv = jnp.concatenate([w_query, w_key, w_value, gains], axis=1)
    eight = ("xh", "core", "head")
    got = lax.all_to_all(jnp.broadcast_to(own_qkv[None], (8, 12, 1920)), eight, 0, 0, tiled=True)
    piece = lax.dynamic_slice_in_dim(got, core * 4, 4, 0).reshape(48, 1920)
    qkv_mine, qkv_other = spread(piece)

    got = lax.all_to_all(jnp.broadcast_to(w_out.T[None], (8, 24, 768)), eight, 0, 0, tiled=True)
    piece = lax.dynamic_slice_in_dim(got, core * 4, 4, 0).reshape(2, 2, 24, 768)
    out_mine, out_other = spread(piece.transpose(0, 2, 1, 3).reshape(48, 1536))

    own_mlp = jnp.stack([w_gate, w_up, w_down.T], axis=1).reshape(24, 3, 2, 1152)
    own_mlp = own_mlp.transpose(2, 0, 1, 3).reshape(2, 1, 24, 3456)
    own_mlp = jnp.broadcast_to(own_mlp, (2, 2, 24, 3456)).reshape(4, 24, 3456)
    got = lax.all_to_all(own_mlp, ("xh", "core"), 0, 0, tiled=True)
    piece = lax.dynamic_slice_in_dim(got, core * 2, 2, 0).reshape(48, 3456)
    mlp_mine, mlp_other = spread(piece)

    cots_own = mixed_order(cotangent)
    cots = jnp.concatenate([cots_own] + [shift_x(cots_own, k) for k in (1, 2, 3)], axis=0)

    gain_table = joined(qkv_mine[:, 1792:1794], qkv_other[:, 1792:1794], 0).astype(F32).T
    first_gain, second_gain = gain_table[0:1], gain_table[1:2]

    inputs = mixed_order(tokens).astype(F32)
    rs1 = lax.rsqrt(jnp.mean(inputs * inputs, axis=-1, keepdims=True) + EPSILON)
    n1 = inputs * rs1
    first_low = (n1 * first_gain).astype(BF)
    first_mine, first_other = halves(first_low, 1)
    projected = (dot(first_mine, qkv_mine[:, :1792]) + dot(first_other, qkv_other[:, :1792])).astype(BF)
    queries = projected[:, :1536]
    keyval_own = projected[:, 1536:]
    earlier = [shift_all(keyval_own[128:], 6)] + [shift_all(keyval_own, k) for k in (5, 4, 3, 2, 1)]
    keyval = jnp.concatenate(earlier + [keyval_own], axis=0)
    attended, probs = attend(block.astype(jnp.int32).reshape(1), queries, keyval)
    branch = joined(dot(attended, out_mine, NT), dot(attended, out_other, NT), 1)
    middle = inputs + branch
    rs2 = lax.rsqrt(jnp.mean(middle * middle, axis=-1, keepdims=True) + EPSILON)
    n2 = middle * rs2
    second_own = (n2 * second_gain).astype(BF)
    seconds = jnp.concatenate([second_own] + [shift_x(second_own, k) for k in (1, 2, 3)], axis=0)

    second_mine, second_other = halves(seconds, 1)
    cots_mine, cots_other = halves(cots, 1)
    gate_up = dot(second_mine, mlp_mine[:, :2304]) + dot(second_other, mlp_other[:, :2304])
    gate, up = gate_up[:, :1152], gate_up[:, 1152:]
    grad_hidden = dot(cots_mine, mlp_mine[:, 2304:]) + dot(cots_other, mlp_other[:, 2304:])

    def geglu(gate_val, up_val):
        return jax.nn.gelu(gate_val, approximate=True) * up_val

    hidden, geglu_back = jax.vjp(geglu, gate, up)
    hidden = hidden.astype(BF)
    grad_gate, grad_up = geglu_back(grad_hidden)
    grad_gate_up = jnp.concatenate([grad_gate, grad_up], axis=1).astype(BF)

    def to_owners(partial):
        pieces = partial.reshape(4, ROW, 1536)
        total = pieces[0].astype(F32)
        for k in (1, 2, 3):
            total = total + shift_x(pieces[k], -k).astype(F32)
        return total

    second_part = joined(dot(grad_gate_up, mlp_mine[:, :2304], NT), dot(grad_gate_up, mlp_other[:, :2304], NT), 1)
    grad_second = to_owners(second_part.astype(BF))
    mlp_part = joined(dot(hidden, mlp_mine[:, 2304:], NT), dot(hidden, mlp_other[:, 2304:], NT), 1)
    block_out = true_order((middle + to_owners(mlp_part.astype(BF))).astype(BF))

    def planes(mine, other):
        total = mine.astype(F32) + swap_core(other.astype(BF)).astype(F32)
        total = total.astype(BF).reshape(16, 48, -1)
        got = lax.all_to_all(total, PLANE, 0, 0, tiled=True)
        return jnp.sum(got.astype(F32), axis=0)

    mlp_grads = []
    for lhs, rhs in (
        ((cots_mine, cots_other), hidden),
        ((second_mine, second_other), grad_gate_up[:, :1152]),
        ((second_mine, second_other), grad_gate_up[:, 1152:]),
    ):
        mlp_grads.append(planes(dot(lhs[0], rhs, TN), dot(lhs[1], rhs, TN)))
    mlp_grads = jnp.concatenate(mlp_grads, axis=1).astype(BF).reshape(1, 2, 24, 3456)
    sent = jnp.broadcast_to(mlp_grads, (2, 2, 24, 3456)).reshape(4, 24, 3456)
    got = lax.all_to_all(sent, ("xh", "core"), 0, 0, tiled=True).reshape(2, 2, 24, 3, 1152)
    got = lax.dynamic_index_in_dim(got, xh, 1, keepdims=False).transpose(2, 1, 0, 3).reshape(3, 24, 2304)
    grad_w_down, grad_w_gate, grad_w_up = got[0].astype(F32).T, got[1].astype(F32), got[2].astype(F32)

    scaled = grad_second * second_gain
    grad_middle = cots_own.astype(F32) + rs2 * (scaled - n2 * jnp.mean(scaled * n2, axis=-1, keepdims=True))
    gain_second_grad = jnp.sum(grad_second * n2, axis=0)
    grad_branch = grad_middle.astype(BF)
    branch_mine, branch_other = halves(grad_branch, 1)
    grad_attended = (dot(branch_mine, out_mine) + dot(branch_other, out_other)).astype(BF)
    out_grads = planes(dot(branch_mine, attended, TN), dot(branch_other, attended, TN))

    def to_eight(grads):
        sent = jnp.where(jnp.arange(2).reshape(2, 1, 1, 1, 1) == core, grads[None], 0.0).astype(BF)
        sent = sent.reshape((8,) + grads.shape[2:])
        return jnp.sum(lax.all_to_all(sent, eight, 0, 0, tiled=True).astype(F32), axis=0)

    grad_w_out = to_eight(out_grads.reshape(2, 24, 2, 768).transpose(0, 2, 1, 3)).T

    dqueries, dkeyval = attend_back(queries, keyval, attended, grad_attended, probs)
    keyval_home = dkeyval[1024:].astype(F32)
    for k in (1, 2, 3, 4, 5):
        start = 1024 - ROW * k
        keyval_home = keyval_home + shift_all(dkeyval[start : start + ROW], -k).astype(F32)
    keyval_home = keyval_home + jnp.pad(shift_all(dkeyval[:64], -6).astype(F32), ((128, 0), (0, 0)))
    dqkv = jnp.concatenate([dqueries, keyval_home.astype(BF)], axis=1)
    grad_first = joined(dot(dqkv, qkv_mine[:, :1792], NT), dot(dqkv, qkv_other[:, :1792], NT), 1)
    scaled = grad_first * first_gain
    input_grad = grad_middle + rs1 * (scaled - n1 * jnp.mean(scaled * n1, axis=-1, keepdims=True))
    input_grad = true_order(input_grad.astype(BF))
    gain_first_grad = jnp.sum(grad_first * n1, axis=0)
    gain_grads = jnp.pad(jnp.stack([gain_first_grad, gain_second_grad], axis=1), ((0, 0), (0, 126)))
    gains_mine, gains_other = halves(gain_grads, 0)
    qkv_grads = planes(
        jnp.concatenate([dot(first_mine, dqkv, TN), gains_mine], axis=1),
        jnp.concatenate([dot(first_other, dqkv, TN), gains_other], axis=1),
    )
    qkv_own = to_eight(qkv_grads.reshape(2, 2, 12, 1920))
    return (
        block_out,
        input_grad,
        qkv_own[:, :1536],
        qkv_own[:, 1536:1664],
        qkv_own[:, 1664:1792],
        grad_w_out,
        grad_w_gate,
        grad_w_up,
        grad_w_down,
        qkv_own[:, 1792],
        qkv_own[:, 1793],
    )


def solution(mesh):
    grid = Mesh(mesh.devices.reshape(SIZES), AXES)
    seq = ("z", "xh", "y", "core")
    rows, both, cols = P(AXES, None), P(seq, "head"), P("head", seq)
    in_specs = (rows, rows, rows, rows, rows, cols, both, both, cols, P(AXES), P(AXES))
    out_specs = (rows, rows, rows, rows, rows, cols, both, both, cols, P(AXES), P(AXES))
    return jax.shard_map(shards, mesh=grid, in_specs=in_specs, out_specs=out_specs, check_vma=False)
```

time: 2240 us -> 646 us (0.29)
  blocking collectives: 1060 us -> 10.3 us
  starting transfers between devices: 353 us -> 107 us
  waiting for transfers between devices: 475 us -> 296 us
  local copies, waits for them, and re-layouts: 143 us -> 56 us
  matrix products: 138 us -> 83.2 us
    all_gather x2 -> x0, blocking collectives: 551 us -> none  [the longest x1 276 us: shards(): lax.all_gather(w_key, ('seq', 'head'), axis=0, tiled=True)]
    unnamed x3 -> x0, blocking collectives: 504 us -> none
    unnamed x96 -> x0, starting transfers between devices: 313 us -> none
    all_gather x6 -> x3, waiting for transfers between devices: 323 us -> 109 us  [spread(): mine = lax.all_gather(piece, PLANE, axis=0, tiled=True)]
    unnamed x122 -> x117, local copies, waits for them, and re-layouts: 136 us -> 13.9 us
    ppermute x6 -> x32, waiting for transfers between devices: 22.3 us -> 103 us  [the longest x12 55.1 us: shift_x(): lax.ppermute(block, CHIPS_X, [(i, (i + distance) % 4) for i in range(4)])]
    psum x2 -> x0, waiting for transfers between devices: 64.4 us -> none  [the longest x1 40.4 us: shards(): lax.psum(second_part.astype(jnp.bfloat16), 'head').astype(jnp.float32)]
    dot_general x24 -> x26, matrix products: 138 us -> 83.2 us  [dot(): return lax.dot_general(a, b, dims, preferred_element_type=F32)]
  transfers between devices with their start and end apart: 119 -> 45, of which waited for: 23 -> 24; matrix products, arithmetic and copies ran while one was open for 30% -> 25% of each run, Pallas kernels for 0% -> 3%
where the time goes in v1:
time: 646 us; the launch traced here: 634 us
  waiting for transfers between devices  296 us (46%)
  starting transfers between devices  107 us (17%)
  matrix products  83.2 us (13%)
  local copies, waits for them, and re-layouts  56 us (9%)
  other arithmetic  45.1 us (7%)
  Pallas kernels  21 us (3%)
  between operations  15.5 us (2%)
  blocking collectives  10.3 us (2%)
    all_gather x3, waiting for transfers between devices, spread(): mine = lax.all_gather(piece, PLANE, axis=0, tiled=True)  109 us
    dot_general x26, matrix products, dot(): return lax.dot_general(a, b, dims, preferred_element_type=F32)  83.2 us
    ppermute x12, waiting for transfers between devices, shift_x(): lax.ppermute(block, CHIPS_X, [(i, (i + distance) % 4) for i in range(4)])  55.1 us
    ppermute x12, waiting for transfers between devices, shift_all(): return lax.ppermute(block, AXES, route)  48 us
    all_to_all x5, waiting for transfers between devices, planes(): got = lax.all_to_all(total, PLANE, 0, 0, tiled=True)  43.4 us
    ppermute x12, starting transfers between devices, shift_all(): return lax.ppermute(block, AXES, route)  35.3 us
    all_to_all x5, starting transfers between devices, planes(): got = lax.all_to_all(total, PLANE, 0, 0, tiled=True)  33.7 us
    ppermute x12, starting transfers between devices, shift_x(): lax.ppermute(block, CHIPS_X, [(i, (i + distance) % 4) for i in range(4)])  17.3 us
  transfers between devices with their start and end apart: 45, of which 24 were waited for; matrix products, arithmetic and copies ran while one was open for 25% of the time, Pallas kernels for 3%

profile of v1, /device:TPU:64, one launch (start us, length us, event | category | flops | bytes accessed | tf_op | source)
XLA Modules:
  0.0 633.9 jit_solution(3999924282713197160)
XLA Ops:
  14.0 9.9 %all-to-all-done = bf16[8,12,1920]{2,1,0:T(8,128)(2,1)S(1)} async-done(((bf16[8,12,1920]{2,1,0:T(8,128)(2,1)}), bf16[8,12,1920]{2,1,0:T(8,128)(2,1)S(1)}, u32[]{:S(2)}, u32[]{:S(2)}) %all-to-all-start) | async-done | bytes 368672 | tf_op jit(solution)/shard_map/all_to_all | solution.py:188
  24.8 10.3 %all_to_all.55 = bf16[8,24,768]{2,1,0:T(8,128)(2,1)S(1)} all-to-all(bf16[8,24,768]{2,1,0:T(8,128)(2,1)S(1)} %broadcast_in_dim.80), channel_id=1, replica_groups=mesh['z'=4,'xh'=2,'y'=4,'core'=2,'head'=2] {'xh','core','head'}, dimensions={0} | all-to-all | bytes 589824 | tf_op jit(solution)/shard_map/all_to_all | solution.py:192
  42.1 11.8 %all-to-all-done.2 = bf16[4,24,3456]{2,1,0:T(8,128)(2,1)S(1)} async-done(((bf16[4,24,3456]{2,1,0:T(8,128)(2,1)}), bf16[4,24,3456]{2,1,0:T(8,128)(2,1)S(1)}, u32[]{:S(2)}, u32[]{:S(2)}) %all-to-all-start.2) | async-done | bytes 663584 | tf_op jit(solution)/shard_map/all_to_all | solution.py:199
  54.6 15.9 %all-gather.4.cloned.1.call-done = bf16[768,1920]{1,0:T(8,128)(2,1)} async-done(((bf16[48,1920]{1,0:T(8,128)(2,1)}), bf16[768,1920]{1,0:T(8,128)(2,1)}) %all-gather.4.cloned.1.call-update) | async-done | bytes 2949136 | tf_op jit(solution)/shard_map/all_gather | solution.py:182
  84.2 34.1 %all-gather.6.cloned.1.call-done = bf16[768,1536]{1,0:T(8,128)(2,1)} async-done(((bf16[48,1536]{1,0:T(8,128)(2,1)}), bf16[768,1536]{1,0:T(8,128)(2,1)}) %all-gather.6.cloned.1.call-update) | async-done | bytes 2359312 | tf_op jit(solution)/shard_map/all_gather | solution.py:182
  119.7 58.6 %all-gather.8.cloned.1.call-done = bf16[768,3456]{1,0:T(8,128)(2,1)} async-done(((bf16[48,3456]{1,0:T(8,128)(2,1)}), bf16[768,3456]{1,0:T(8,128)(2,1)}) %all-gather.8.cloned.1.call-update) | async-done | bytes 5308432 | tf_op jit(solution)/shard_map/all_gather | solution.py:182
  189.0 5.0 collective-permute-done.1
  197.0 8.0 %collective-permute-done.2 = bf16[192,256]{1,0:T(8,128)(2,1)S(1)} collective-permute-done((bf16[192,256]{1,0:T(8,128)(2,1)S(1)}, bf16[192,256]{1,0:T(8,128)(2,1)S(1)}, u32[]{:S(2)}, u32[]{:S(2)}) %collective-permute-start.2) | collective-permute-done | bytes 98336 | tf_op jit(solution)/shard_map/ppermute | solution.py:143
  207.0 9.4 %collective-permute-done.3 = bf16[192,256]{1,0:T(8,128)(2,1)S(1)} collective-permute-done((bf16[192,256]{1,0:T(8,128)(2,1)S(1)}, bf16[192,256]{1,0:T(8,128)(2,1)S(1)}, u32[]{:S(2)}, u32[]{:S(2)}) %collective-permute-start.3) | collective-permute-done | bytes 98336 | tf_op jit(solution)/shard_map/ppermute | solution.py:143
  218.3 8.8 %collective-permute-done.4 = bf16[192,256]{1,0:T(8,128)(2,1)S(1)} collective-permute-done((bf16[192,256]{1,0:T(8,128)(2,1)S(1)}, bf16[192,256]{1,0:T(8,128)(2,1)S(1)}, u32[]{:S(2)}, u32[]{:S(2)}) %collective-permute-start.4) | collective-permute-done | bytes 98336 | tf_op jit(solution)/shard_map/ppermute | solution.py:143
  229.1 8.5 %collective-permute-done.5 = bf16[192,256]{1,0:T(8,128)(2,1)S(1)} collective-permute-done((bf16[192,256]{1,0:T(8,128)(2,1)S(1)}, bf16[192,256]{1,0:T(8,128)(2,1)S(1)}, u32[]{:S(2)}, u32[]{:S(2)}) %collective-permute-start.5) | collective-permute-done | bytes 98336 | tf_op jit(solution)/shard_map/ppermute | solution.py:143
  239.5 8.2 %collective-permute-done.6 = bf16[192,256]{1,0:T(8,128)(2,1)S(1)} collective-permute-done((bf16[192,256]{1,0:T(8,128)(2,1)S(1)}, bf16[192,256]{1,0:T(8,128)(2,1)S(1)}, u32[]{:S(2)}, u32[]{:S(2)}) %collective-permute-start.6) | collective-permute-done | bytes 98336 | tf_op jit(solution)/shard_map/ppermute | solution.py:143
  248.6 10.3 %attend.1 = (bf16[192,1536]{1,0:T(8,128)(2,1)}, bf16[6,1216,384]{2,1,0:T(8,128)(2,1)}) custom-call(s32[1]{0:T(128)} %bitcast.2.block_ref, bf16[192,1536]{1,0:T(8,128)(2,1)} %slice.183.q_ref, bf16[1216,256]{1,0:T(8,128)(2,1)} %copy-done.44), custom_call_target="tpu_custom_call" | custom-call | flops 1434451968 | bytes 8388608 | tf_op jit(solution)/shard_map/attend/pallas_call | solution.py:62
  287.2 6.2 collective-permute-done.8
  295.2 5.8 fusion.13
  307.5 6.2 fusion.7
  319.0 5.0 select_convert_fusion.1
  336.0 17.8 %collective-permute-done.20 = bf16[192,1536]{1,0:T(8,128)(2,1)S(1)} collective-permute-done((bf16[192,1536]{1,0:T(8,128)(2,1)S(1)}, bf16[192,1536]{1,0:T(8,128)(2,1)S(1)}, u32[]{:S(2)}, u32[]{:S(2)}) %collective-permute-start.20) | collective-permute-done | bytes 589856 | tf_op jit(solution)/shard_map/ppermute | solution.py:147
  359.0 6.6 %all-to-all-start.9 = ((bf16[16,48,1152]{2,1,0:T(8,128)(2,1)}), bf16[16,48,1152]{2,1,0:T(8,128)(2,1)}, u32[]{:S(2)}, u32[]{:S(2)}) async-start(bf16[16,48,1152]{2,1,0:T(8,128)(2,1)} %bitcast.94), calls=%async_computation.9 | async-start | bytes 3538944 | tf_op jit(solution)/shard_map/all_to_all | solution.py:256
  371.7 10.6 %attend_back.1 = (bf16[192,1536]{1,0:T(8,128)(2,1)}, bf16[1216,256]{1,0:T(8,128)(2,1)}) custom-call(bf16[192,1536]{1,0:T(8,128)(2,1)} %slice.183.q_ref, bf16[1216,256]{1,0:T(8,128)(2,1)} %copy-done.44, bf16[192,1536]{1,0:T(8,128)(2,1)} %get-tuple-element.15.out_ref, bf16[192,1536]{1,0:T(8,128)(2,1)} %fusion.18.grad_ref, ...), custom_call_target="tpu_custom_call" | custom-call | flops 2868903936 | bytes 9437184 | tf_op jit(solution)/shard_map/attend_back/pallas_call | solution.py:120
  384.9 5.4 collective-permute-start.25
  412.0 5.0 all-to-all-start.8
  434.9 5.3 fusion.8
  440.3 4.6 all-to-all-done.8
  444.9 7.8 %all-to-all-start.7 = ((bf16[16,48,1152]{2,1,0:T(8,128)(2,1)}), bf16[16,48,1152]{2,1,0:T(8,128)(2,1)}, u32[]{:S(2)}, u32[]{:S(2)}) async-start(bf16[16,48,1152]{2,1,0:T(8,128)(2,1)} %bitcast.95), calls=%async_computation.7 | async-start | bytes 3538944 | tf_op jit(solution)/shard_map/all_to_all | solution.py:256
  467.4 10.5 %all-to-all-done.7 = bf16[16,48,1152]{2,1,0:T(8,128)(2,1)} async-done(((bf16[16,48,1152]{2,1,0:T(8,128)(2,1)}), bf16[16,48,1152]{2,1,0:T(8,128)(2,1)}, u32[]{:S(2)}, u32[]{:S(2)}) %all-to-all-start.7) | async-done | bytes 1769504 | tf_op jit(solution)/shard_map/all_to_all | solution.py:256
  490.2 8.0 %all-to-all-done.10 = bf16[4,24,3456]{2,1,0:T(8,128)(2,1)} async-done(((bf16[4,24,3456]{2,1,0:T(8,128)(2,1)}), bf16[4,24,3456]{2,1,0:T(8,128)(2,1)}, u32[]{:S(2)}, u32[]{:S(2)}) %all-to-all-start.10) | async-done | bytes 663584 | tf_op jit(solution)/shard_map/all_to_all | solution.py:268
  498.3 7.1 %all-to-all-start.5 = ((bf16[16,48,1536]{2,1,0:T(8,128)(2,1)}), bf16[16,48,1536]{2,1,0:T(8,128)(2,1)}, u32[]{:S(2)}, u32[]{:S(2)}) async-start(bf16[16,48,1536]{2,1,0:T(8,128)(2,1)} %bitcast.87), calls=%async_computation.5 | async-start | bytes 4718592 | tf_op jit(solution)/shard_map/all_to_all | solution.py:256
  510.3 28.3 %all-to-all-done.5 = bf16[16,48,1536]{2,1,0:T(8,128)(2,1)} async-done(((bf16[16,48,1536]{2,1,0:T(8,128)(2,1)}), bf16[16,48,1536]{2,1,0:T(8,128)(2,1)}, u32[]{:S(2)}, u32[]{:S(2)}) %all-to-all-start.5) | async-done | bytes 2359328 | tf_op jit(solution)/shard_map/all_to_all | solution.py:256
  538.6 7.3 %all-to-all-start.3 = ((bf16[16,48,1920]{2,1,0:T(8,128)(2,1)}), bf16[16,48,1920]{2,1,0:T(8,128)(2,1)}, u32[]{:S(2)}, u32[]{:S(2)}) async-start(bf16[16,48,1920]{2,1,0:T(8,128)(2,1)} %bitcast.86), calls=%async_computation.3 | async-start | bytes 5898240 | tf_op jit(solution)/shard_map/all_to_all | solution.py:256
  559.4 23.5 %collective-permute-done.14 = bf16[192,1536]{1,0:T(8,128)(2,1)} collective-permute-done((bf16[192,1536]{1,0:T(8,128)(2,1)}, bf16[192,1536]{1,0:T(8,128)(2,1)}, u32[]{:S(2)}, u32[]{:S(2)}) %collective-permute-start.14) | collective-permute-done | bytes 589856 | tf_op jit(solution)/shard_map/ppermute | solution.py:147
  617.9 6.7 %all-to-all-done.4 = bf16[8,12,1920]{2,1,0:T(8,128)(2,1)S(1)} async-done(((bf16[8,12,1920]{2,1,0:T(8,128)(2,1)}), bf16[8,12,1920]{2,1,0:T(8,128)(2,1)S(1)}, u32[]{:S(2)}, u32[]{:S(2)}) %all-to-all-start.4) | async-done | bytes 368672 | tf_op jit(solution)/shard_map/all_to_all | solution.py:283
  (307 shorter events, 242.0 us)
Async XLA Ops:
  13.9 56.6 %all-gather.4.cloned.1.call-start = ((), (), s32[]{:S(2)}) async-start(), calls=%async_computation.11 | async-start | bytes 3133440 | tf_op jit(solution)/shard_map/all_gather | solution.py:182
  24.7 93.6 %all-gather.6.cloned.1.call-start = ((), (), s32[]{:S(2)}) async-start(), calls=%async_computation.12 | async-start | bytes 2506752 | tf_op jit(solution)/shard_map/all_gather | solution.py:182
  42.0 136.2 %all-gather.8.cloned.1.call-start = ((), (), s32[]{:S(2)}) async-start(), calls=%async_computation.13 | async-start | bytes 5640192 | tf_op jit(solution)/shard_map/all_gather | solution.py:182
  70.6 47.8 %collective-permute-start = (bf16[768,1920]{1,0:T(8,128)(2,1)}, bf16[768,1920]{1,0:T(8,128)(2,1)}, u32[]{:S(2)}, u32[]{:S(2)}) collective-permute-start(bf16[768,1920]{1,0:T(8,128)(2,1)} %all-gather.4.cloned.1.call-done), channel_id=1, source_target_pairs={{0,2},{2,0},{1,3},{3,1},{4,6},{6,4},{5,7},{7,5},{8,10},{10,8},{9,1... | collective-permute-start | bytes 8847368 | tf_op jit(solution)/shard_map/ppermute | solution.py:151
  73.4 197.2 %collective-permute-start.15 = (bf16[192,1536]{1,0:T(8,128)(2,1)}, bf16[192,1536]{1,0:T(8,128)(2,1)}, u32[]{:S(2)}, u32[]{:S(2)}) collective-permute-start(bf16[192,1536]{1,0:T(8,128)(2,1)} %reshape.229), channel_id=1, source_target_pairs={{0,1},{1,16},{16,17},{17,0},{2,3},{3,18},{18,19},{19,2},{4,5},{5,2... | collective-permute-start | bytes 1769480 | tf_op jit(solution)/shard_map/ppermute | solution.py:147
  74.8 199.9 %collective-permute-start.16 = (bf16[192,1536]{1,0:T(8,128)(2,1)}, bf16[192,1536]{1,0:T(8,128)(2,1)}, u32[]{:S(2)}, u32[]{:S(2)}) collective-permute-start(bf16[192,1536]{1,0:T(8,128)(2,1)} %reshape.229), channel_id=1, source_target_pairs={{0,16},{1,17},{16,0},{17,1},{2,18},{3,19},{18,2},{19,3},{4,20},{5,... | collective-permute-start | bytes 1769480 | tf_op jit(solution)/shard_map/ppermute | solution.py:147
  118.3 140.6 %collective-permute-start.7 = (bf16[768,1536]{1,0:T(8,128)(2,1)}, bf16[768,1536]{1,0:T(8,128)(2,1)}, u32[]{:S(2)}, u32[]{:S(2)}) collective-permute-start(bf16[768,1536]{1,0:T(8,128)(2,1)} %all-gather.6.cloned.1.call-done), channel_id=1, source_target_pairs={{0,2},{2,0},{1,3},{3,1},{4,6},{6,4},{5,7},{7,5},{8,10},{10,8},{9,1... | collective-permute-start | bytes 7077896 | tf_op jit(solution)/shard_map/ppermute | solution.py:151
  178.2 116.9 %collective-permute-start.11 = (bf16[768,3456]{1,0:T(8,128)(2,1)}, bf16[768,3456]{1,0:T(8,128)(2,1)}, u32[]{:S(2)}, u32[]{:S(2)}) collective-permute-start(bf16[768,3456]{1,0:T(8,128)(2,1)} %all-gather.8.cloned.1.call-done), channel_id=1, source_target_pairs={{0,2},{2,0},{1,3},{3,1},{4,6},{6,4},{5,7},{7,5},{8,10},{10,8},{9,1... | collective-permute-start | bytes 15925256 | tf_op jit(solution)/shard_map/ppermute | solution.py:151
  247.7 31.0 %collective-permute-start.17 = (bf16[192,1536]{1,0:T(8,128)(2,1)}, bf16[192,1536]{1,0:T(8,128)(2,1)}, u32[]{:S(2)}, u32[]{:S(2)}) collective-permute-start(bf16[192,1536]{1,0:T(8,128)(2,1)} %reshape.229), channel_id=1, source_target_pairs={{0,17},{1,0},{16,1},{17,16},{2,19},{3,2},{18,3},{19,18},{4,21},{5,... | collective-permute-start | bytes 1769480 | tf_op jit(solution)/shard_map/ppermute | solution.py:147
  270.6 16.6 %collective-permute-start.9 = (bf16[192,1536]{1,0:T(8,128)(2,1)}, bf16[192,1536]{1,0:T(8,128)(2,1)}, u32[]{:S(2)}, u32[]{:S(2)}) collective-permute-start(bf16[192,1536]{1,0:T(8,128)(2,1)} %get-tuple-element.28), channel_id=1, source_target_pairs={{0,16},{1,17},{16,0},{17,1},{2,18},{3,19},{18,2},{19,3},{4,20},{5,... | collective-permute-start | bytes 1769480 | tf_op jit(solution)/shard_map/ppermute | solution.py:147
  274.7 18.7 %collective-permute-start.8 = (bf16[192,1536]{1,0:T(8,128)(2,1)}, bf16[192,1536]{1,0:T(8,128)(2,1)}, u32[]{:S(2)}, u32[]{:S(2)}) collective-permute-start(bf16[192,1536]{1,0:T(8,128)(2,1)} %get-tuple-element.28), channel_id=1, source_target_pairs={{0,1},{1,16},{16,17},{17,0},{2,3},{3,18},{18,19},{19,2},{4,5},{5,2... | collective-permute-start | bytes 1769480 | tf_op jit(solution)/shard_map/ppermute | solution.py:147
  315.5 40.4 %collective-permute-start.31 = (bf16[768,1152]{1,0:T(8,128)(2,1)S(1)}, bf16[768,1152]{1,0:T(8,128)(2,1)S(1)}, u32[]{:S(2)}, u32[]{:S(2)}) collective-permute-start(bf16[768,1152]{1,0:T(8,128)(2,1)S(1)} %convolution_convert_fusion.2), channel_id=1, source_target_pairs={{0,2},{2,0},{1,3},{3,1},{4,6},{6,4},{5,7},{7,5},{8,10},{10,8},{9,1... | collective-permute-start | bytes 5308424 | tf_op jit(solution)/shard_map/ppermute | solution.py:151
  324.1 29.6 %collective-permute-start.20 = (bf16[192,1536]{1,0:T(8,128)(2,1)S(1)}, bf16[192,1536]{1,0:T(8,128)(2,1)S(1)}, u32[]{:S(2)}, u32[]{:S(2)}) collective-permute-start(bf16[192,1536]{1,0:T(8,128)(2,1)S(1)} %get-tuple-element.36), channel_id=1, source_target_pairs={{0,1},{1,16},{16,17},{17,0},{2,3},{3,18},{18,19},{19,2},{4,5},{5,2... | collective-permute-start | bytes 1769480 | tf_op jit(solution)/shard_map/ppermute | solution.py:147
  325.4 28.4 %collective-permute-start.19 = (bf16[192,1536]{1,0:T(8,128)(2,1)S(1)}, bf16[192,1536]{1,0:T(8,128)(2,1)S(1)}, u32[]{:S(2)}, u32[]{:S(2)}) collective-permute-start(bf16[192,1536]{1,0:T(8,128)(2,1)S(1)} %get-tuple-element.37), channel_id=1, source_target_pairs={{0,16},{1,17},{16,0},{17,1},{2,18},{3,19},{18,2},{19,3},{4,20},{5,... | collective-permute-start | bytes 1769480 | tf_op jit(solution)/shard_map/ppermute | solution.py:147
  326.3 28.1 %collective-permute-start.18 = (bf16[192,1536]{1,0:T(8,128)(2,1)S(1)}, bf16[192,1536]{1,0:T(8,128)(2,1)S(1)}, u32[]{:S(2)}, u32[]{:S(2)}) collective-permute-start(bf16[192,1536]{1,0:T(8,128)(2,1)S(1)} %get-tuple-element.35), channel_id=1, source_target_pairs={{0,17},{1,0},{16,1},{17,16},{2,19},{3,2},{18,3},{19,18},{4,21},{5,... | collective-permute-start | bytes 1769480 | tf_op jit(solution)/shard_map/ppermute | solution.py:147
  331.7 64.5 %collective-permute-start.30 = (bf16[768,1152]{1,0:T(8,128)(2,1)}, bf16[768,1152]{1,0:T(8,128)(2,1)}, u32[]{:S(2)}, u32[]{:S(2)}) collective-permute-start(bf16[768,1152]{1,0:T(8,128)(2,1)} %convolution_convert_fusion.3), channel_id=1, source_target_pairs={{0,2},{2,0},{1,3},{3,1},{4,6},{6,4},{5,7},{7,5},{8,10},{10,8},{9,1... | collective-permute-start | bytes 5308424 | tf_op jit(solution)/shard_map/ppermute | solution.py:151
  353.7 81.2 %collective-permute-start.29 = (bf16[768,1152]{1,0:T(8,128)(2,1)}, bf16[768,1152]{1,0:T(8,128)(2,1)}, u32[]{:S(2)}, u32[]{:S(2)}) collective-permute-start(bf16[768,1152]{1,0:T(8,128)(2,1)} %convolution_convert_fusion.4), channel_id=1, source_target_pairs={{0,2},{2,0},{1,3},{3,1},{4,6},{6,4},{5,7},{7,5},{8,10},{10,8},{9,1... | collective-permute-start | bytes 5308424 | tf_op jit(solution)/shard_map/ppermute | solution.py:151
  359.0 53.0 %all-to-all-start.9 = ((bf16[16,48,1152]{2,1,0:T(8,128)(2,1)}), bf16[16,48,1152]{2,1,0:T(8,128)(2,1)}, u32[]{:S(2)}, u32[]{:S(2)}) async-start(bf16[16,48,1152]{2,1,0:T(8,128)(2,1)} %bitcast.94), calls=%async_computation.9 | async-start | bytes 3538944 | tf_op jit(solution)/shard_map/all_to_all | solution.py:256
  384.9 24.1 %collective-permute-start.25 = (bf16[192,256]{1,0:T(8,128)(2,1)S(1)}, bf16[192,256]{1,0:T(8,128)(2,1)S(1)}, u32[]{:S(2)}, u32[]{:S(2)}) collective-permute-start(bf16[192,256]{1,0:T(8,128)(2,1)S(1)} %get-tuple-element.52), channel_id=1, source_target_pairs={{5,0},{6,1},{7,2},{8,3},{9,4},{10,5},{11,6},{12,7},{13,8},{14,9},{... | collective-permute-start | bytes 294920 | tf_op jit(solution)/shard_map/ppermute | solution.py:143
  390.4 30.5 %collective-permute-start.24 = (bf16[192,256]{1,0:T(8,128)(2,1)}, bf16[192,256]{1,0:T(8,128)(2,1)S(1)}, u32[]{:S(2)}, u32[]{:S(2)}) collective-permute-start(bf16[192,256]{1,0:T(8,128)(2,1)} %get-tuple-element.53), channel_id=1, source_target_pairs={{4,0},{5,1},{6,2},{7,3},{8,4},{9,5},{10,6},{11,7},{12,8},{13,9},{1... | collective-permute-start | bytes 294920 | tf_op jit(solution)/shard_map/ppermute | solution.py:143
  394.3 27.0 %collective-permute-start.23 = (bf16[192,256]{1,0:T(8,128)(2,1)}, bf16[192,256]{1,0:T(8,128)(2,1)}, u32[]{:S(2)}, u32[]{:S(2)}) collective-permute-start(bf16[192,256]{1,0:T(8,128)(2,1)} %get-tuple-element.54), channel_id=1, source_target_pairs={{3,0},{4,1},{5,2},{6,3},{7,4},{8,5},{9,6},{10,7},{11,8},{12,9},{13... | collective-permute-start | bytes 294920 | tf_op jit(solution)/shard_map/ppermute | solution.py:143
  405.0 16.3 %collective-permute-start.22 = (bf16[192,256]{1,0:T(8,128)(2,1)}, bf16[192,256]{1,0:T(8,128)(2,1)}, u32[]{:S(2)}, u32[]{:S(2)}) collective-permute-start(bf16[192,256]{1,0:T(8,128)(2,1)} %get-tuple-element.55), channel_id=1, source_target_pairs={{2,0},{3,1},{4,2},{5,3},{6,4},{7,5},{8,6},{9,7},{10,8},{11,9},{12,... | collective-permute-start | bytes 294920 | tf_op jit(solution)/shard_map/ppermute | solution.py:143
  412.0 32.9 %all-to-all-start.8 = ((bf16[16,48,1152]{2,1,0:T(8,128)(2,1)}), bf16[16,48,1152]{2,1,0:T(8,128)(2,1)}, u32[]{:S(2)}, u32[]{:S(2)}) async-start(bf16[16,48,1152]{2,1,0:T(8,128)(2,1)} %bitcast.93), calls=%async_computation.8 | async-start | bytes 3538944 | tf_op jit(solution)/shard_map/all_to_all | solution.py:256
  420.8 65.5 %collective-permute-start.28 = (bf16[768,1536]{1,0:T(8,128)(2,1)}, bf16[768,1536]{1,0:T(8,128)(2,1)}, u32[]{:S(2)}, u32[]{:S(2)}) collective-permute-start(bf16[768,1536]{1,0:T(8,128)(2,1)} %convolution_convert_fusion), channel_id=1, source_target_pairs={{0,2},{2,0},{1,3},{3,1},{4,6},{6,4},{5,7},{7,5},{8,10},{10,8},{9,1... | collective-permute-start | bytes 7077896 | tf_op jit(solution)/shard_map/ppermute | solution.py:151
  444.9 33.0 %all-to-all-start.7 = ((bf16[16,48,1152]{2,1,0:T(8,128)(2,1)}), bf16[16,48,1152]{2,1,0:T(8,128)(2,1)}, u32[]{:S(2)}, u32[]{:S(2)}) async-start(bf16[16,48,1152]{2,1,0:T(8,128)(2,1)} %bitcast.95), calls=%async_computation.7 | async-start | bytes 3538944 | tf_op jit(solution)/shard_map/all_to_all | solution.py:256
  463.9 42.4 %collective-permute-start.27 = (bf16[768,1920]{1,0:T(8,128)(2,1)}, bf16[768,1920]{1,0:T(8,128)(2,1)}, u32[]{:S(2)}, u32[]{:S(2)}) collective-permute-start(bf16[768,1920]{1,0:T(8,128)(2,1)} %pad_maximum_fusion.1), channel_id=1, source_target_pairs={{0,2},{2,0},{1,3},{3,1},{4,6},{6,4},{5,7},{7,5},{8,10},{10,8},{9,1... | collective-permute-start | bytes 8847368 | tf_op jit(solution)/shard_map/ppermute | solution.py:151
  482.2 16.1 %all-to-all-start.10 = ((bf16[4,24,3456]{2,1,0:T(8,128)(2,1)}), bf16[4,24,3456]{2,1,0:T(8,128)(2,1)}, u32[]{:S(2)}, u32[]{:S(2)}) async-start(bf16[4,24,3456]{2,1,0:T(8,128)(2,1)} %bitcast.92), calls=%async_computation.10 | async-start | bytes 1327104 | tf_op jit(solution)/shard_map/all_to_all | solution.py:268
  498.3 40.3 %all-to-all-start.5 = ((bf16[16,48,1536]{2,1,0:T(8,128)(2,1)}), bf16[16,48,1536]{2,1,0:T(8,128)(2,1)}, u32[]{:S(2)}, u32[]{:S(2)}) async-start(bf16[16,48,1536]{2,1,0:T(8,128)(2,1)} %bitcast.87), calls=%async_computation.5 | async-start | bytes 4718592 | tf_op jit(solution)/shard_map/all_to_all | solution.py:256
  538.6 60.9 %all-to-all-start.3 = ((bf16[16,48,1920]{2,1,0:T(8,128)(2,1)}), bf16[16,48,1920]{2,1,0:T(8,128)(2,1)}, u32[]{:S(2)}, u32[]{:S(2)}) async-start(bf16[16,48,1920]{2,1,0:T(8,128)(2,1)} %bitcast.86), calls=%async_computation.3 | async-start | bytes 5898240 | tf_op jit(solution)/shard_map/all_to_all | solution.py:256
  555.0 27.9 %collective-permute-start.14 = (bf16[192,1536]{1,0:T(8,128)(2,1)}, bf16[192,1536]{1,0:T(8,128)(2,1)}, u32[]{:S(2)}, u32[]{:S(2)}) collective-permute-start(bf16[192,1536]{1,0:T(8,128)(2,1)} %get-tuple-element.41), channel_id=1, source_target_pairs={{0,1},{1,16},{16,17},{17,0},{2,3},{3,18},{18,19},{19,2},{4,5},{5,2... | collective-permute-start | bytes 1769480 | tf_op jit(solution)/shard_map/ppermute | solution.py:147
  555.0 27.9 %collective-permute-start.13 = (bf16[192,1536]{1,0:T(8,128)(2,1)}, bf16[192,1536]{1,0:T(8,128)(2,1)}, u32[]{:S(2)}, u32[]{:S(2)}) collective-permute-start(bf16[192,1536]{1,0:T(8,128)(2,1)} %get-tuple-element.42), channel_id=1, source_target_pairs={{0,16},{1,17},{16,0},{17,1},{2,18},{3,19},{18,2},{19,3},{4,20},{5,... | collective-permute-start | bytes 1769480 | tf_op jit(solution)/shard_map/ppermute | solution.py:147
  556.4 27.2 %collective-permute-start.12 = (bf16[192,1536]{1,0:T(8,128)(2,1)}, bf16[192,1536]{1,0:T(8,128)(2,1)}, u32[]{:S(2)}, u32[]{:S(2)}) collective-permute-start(bf16[192,1536]{1,0:T(8,128)(2,1)} %get-tuple-element.40), channel_id=1, source_target_pairs={{0,17},{1,0},{16,1},{17,16},{2,19},{3,2},{18,3},{19,18},{4,21},{5,... | collective-permute-start | bytes 1769480 | tf_op jit(solution)/shard_map/ppermute | solution.py:147
  (64 other events, 1333.3 us)
Sparse Core Ops, SparseCore 0:
  24.8 45.6 all-gather.3
  73.3 45.0 all-gather.5
  121.1 57.1 all-gather.7

commit v2 on v1

v2 whole, which is shorter than its diff:
```python
import functools
import jax
import jax.numpy as jnp
from jax import lax
from jax.experimental import pallas as pl
from jax.experimental.pallas import tpu as pltpu
from jax.sharding import Mesh
from jax.sharding import PartitionSpec as P

WINDOW = 1024
EPSILON = 1e-06
AXES = ("z", "xh", "y", "core", "head")
SIZES = (4, 2, 4, 2, 2)
CHIPS_X = ("xh", "head")
PLANE = ("z", "y")
ROW = 192
KEYS = 1216
HEADS = 12
HD = 128
BF = jnp.bfloat16
F32 = jnp.float32
NEG = -1e30
SCALE = HD ** (-0.5)
LOG2E = 1.4426950408889634
VMEM_BYTES = 56 * 1024 * 1024
FF = 1152
FF_TILES = 3
FF_TILE = 384
RING = 768
GELU_A = 0.7978845608028654
GELU_B = GELU_A * 0.044715

NN = (((1,), (0,)), ((), ()))
NT = (((1,), (1,)), ((), ()))
TN = (((0,), (0,)), ((), ()))


def dot(a, b, dims=NN):
    return lax.dot_general(a, b, dims, preferred_element_type=F32)


ANY = pl.BlockSpec(memory_space=pl.ANY)


def cost(micros):
    return pl.CostEstimate(flops=int(micros * 1.0e9), bytes_accessed=1000000, transcendentals=0)


def call(kernel, name, outs, args, needs=(), micros=0.01, grid=None, in_specs=None, out_specs=None, scratch=(), scalars=0):
    count = len(args)

    def body(*refs):
        kernel(*refs[:count], *refs[count + len(needs) :])

    if in_specs is None:
        whole = pl.BlockSpec(memory_space=pltpu.VMEM)
        in_specs = [pl.BlockSpec(memory_space=pltpu.SMEM)] * scalars + [whole] * (count - scalars)
        out_specs = [whole] * len(outs)
        spec = dict(in_specs=in_specs + [ANY] * len(needs), out_specs=out_specs, scratch_shapes=list(scratch))
    else:
        spec = dict(
            grid_spec=pltpu.PrefetchScalarGridSpec(
                num_scalar_prefetch=scalars,
                grid=grid,
                in_specs=in_specs + [ANY] * len(needs),
                out_specs=out_specs,
                scratch_shapes=list(scratch),
            )
        )
    return pl.pallas_call(
        body,
        out_shape=[jax.ShapeDtypeStruct(shape, kind) for shape, kind in outs],
        compiler_params=pltpu.CompilerParams(vmem_limit_bytes=VMEM_BYTES),
        cost_estimate=cost(micros),
        name=name,
        **spec,
    )(*args, *needs)


def after(values, *needs):
    count = len(values)
    return pl.pallas_call(
        lambda *refs: None,
        in_specs=[ANY] * (count + len(needs)),
        out_specs=[ANY] * count,
        out_shape=[jax.ShapeDtypeStruct(value.shape, value.dtype) for value in values],
        input_output_aliases={i: i for i in range(count)},
        cost_estimate=cost(0.01),
        name="after",
    )(*values, *needs)


def two_heads(pair):
    return jnp.concatenate([pair[:, :HD], pair[:, HD:]], axis=0)


def attend_kernel(place_ref, q_ref, far_ref, near_ref, here_ref, out_ref, probs_ref, kv_ref, bias, table):
    @pl.when(pl.program_id(0) == 0)
    def _():
        key = lax.broadcasted_iota(jnp.int32, (KEYS, ROW), 0)
        query = lax.broadcasted_iota(jnp.int32, (KEYS, ROW), 1)
        first = WINDOW - ROW * place_ref[0]
        inside = (key > query) & (key <= query + WINDOW) & (key >= first)
        one = jnp.where(inside, 0.0, NEG)
        bias[:, :] = jnp.concatenate([one, one], axis=1)
        table[:256, :] = far_ref[...]
        table[256:1024, :] = near_ref[...]
        table[1024:, :] = here_ref[...]
        kv_ref[...] = table[pl.ds(pl.multiple_of(place_ref[1] * ROW, ROW), KEYS), :]

    queries = two_heads(q_ref[...])
    scores = dot(kv_ref[:, :HD], queries, NT) + bias[...]
    highest = jnp.max(scores, axis=0, keepdims=True)
    powers = jnp.exp2((scores - highest) * (SCALE * LOG2E))
    total = jnp.sum(powers, axis=0, keepdims=True)
    probs = (powers * (1.0 / total)).astype(BF)
    probs_ref[0] = probs
    mixed = dot(kv_ref[:, HD:], probs, TN).T.astype(BF)
    out_ref[...] = jnp.concatenate([mixed[:ROW], mixed[ROW:]], axis=1)


def attend(place, queries, far, near, here, needs):
    pair = pl.BlockSpec((ROW, 2 * HD), lambda h, b: (0, h))

    def fixed(rows):
        return pl.BlockSpec((rows, 2 * HD), lambda h, b: (0, 0))

    return call(
        attend_kernel,
        "attend",
        [((ROW, HEADS * HD), BF), ((HEADS // 2, KEYS, 2 * ROW), BF), ((KEYS, 2 * HD), BF)],
        [place, queries, far, near, here],
        needs=needs,
        grid=(HEADS // 2,),
        in_specs=[pair, fixed(256), fixed(768), fixed(768)],
        out_specs=[pair, pl.BlockSpec((1, KEYS, 2 * ROW), lambda h, b: (h, 0, 0)), fixed(KEYS)],
        scratch=[pltpu.VMEM((KEYS, 2 * ROW), F32), pltpu.VMEM((1792, 2 * HD), BF)],
        scalars=1,
    )


HOME_ROWS = [slice(0, 64)] + [slice(64 + ROW * i, 64 + ROW * (i + 1)) for i in range(6)]


def attend_back_kernel(q_ref, kv_ref, out_ref, grad_ref, probs_ref, dq_ref, *rest):
    homes, (dk, dv) = rest[:7], rest[7:]
    step = pl.program_id(0)

    @pl.when(step == 0)
    def _():
        dk[...] = jnp.zeros_like(dk)
        dv[...] = jnp.zeros_like(dv)

    queries = two_heads(q_ref[...])
    grads = two_heads(grad_ref[...])
    outs = two_heads(out_ref[...])
    probs = probs_ref[0]
    delta = jnp.sum((grads.astype(F32) * outs.astype(F32)).T, axis=0, keepdims=True)
    dprobs = dot(kv_ref[:, HD:], grads, NT)
    dscores = (probs.astype(F32) * (dprobs - delta)).astype(BF)
    dqueries = (dot(kv_ref[:, :HD], dscores, TN).T * SCALE).astype(BF)
    dq_ref[...] = jnp.concatenate([dqueries[:ROW], dqueries[ROW:]], axis=1)
    dk[...] += dot(dscores, queries)
    dv[...] += dot(probs, grads)

    @pl.when(step == HEADS // 2 - 1)
    def _():
        for home, rows in zip(homes, HOME_ROWS):
            home[:, :HD] = (dk[rows, :] * SCALE).astype(BF)
            home[:, HD:] = dv[rows, :].astype(BF)


def attend_back(queries, keyval, attended, grads, probs, needs):
    pair = pl.BlockSpec((ROW, 2 * HD), lambda h: (0, h))
    table = pl.BlockSpec((KEYS, 2 * HD), lambda h: (0, 0))

    def home(rows):
        return pl.BlockSpec((rows, 2 * HD), lambda h: (0, 0))

    return call(
        attend_back_kernel,
        "attend_back",
        [((ROW, HEADS * HD), BF), ((64, 2 * HD), BF)] + [((ROW, 2 * HD), BF)] * 6,
        [queries, keyval, attended, grads, probs],
        needs=needs,
        micros=6.0,
        grid=(HEADS // 2,),
        in_specs=[pair, table, pair, pair, pl.BlockSpec((1, KEYS, 2 * ROW), lambda h: (h, 0, 0))],
        out_specs=[pair, home(64)] + [home(ROW)] * 6,
        scratch=[pltpu.VMEM((KEYS, HD), F32), pltpu.VMEM((KEYS, HD), F32)],
    )


def ring_rows(ring, back):
    return pl.ds(pl.multiple_of(lax.rem(ring + 4 - back, 4) * ROW, ROW), ROW)


BACKS = (0, 1, 3, 2)


def mlp_kernel(
    ring_ref, zero, one, three, two, cots, pair_a, pair_b, down_a, down_b, hidden_ref, dpair_ref, rows, rows_b, second_ref,
    second_sum
):
    @pl.when(pl.program_id(0) == 0)
    def _():
        for block, back in zip((zero, one, three, two), BACKS):
            rows[ring_rows(ring_ref[0], back), :] = block[...]
            rows_b[ring_rows(ring_ref[0], back), :] = block[:, 768:]

    step = pl.program_id(0)
    low, high = slice(0, 768), slice(768, 1536)
    both = dot(rows[:, low], pair_a[...]) + dot(rows[:, high], pair_b[...])
    gate, up = both[:, :FF_TILE], both[:, FF_TILE:]
    dhidden = dot(cots[:, low], down_a[...]) + dot(cots[:, high], down_b[...])
    square = gate * gate
    wave = jnp.tanh(gate * (GELU_A + GELU_B * square))
    half = 0.5 + 0.5 * wave
    gelu = gate * half
    slope = half + gate * (0.5 - 0.5 * wave * wave) * (GELU_A + 3.0 * GELU_B * square)
    hidden_ref[...] = (gelu * up).astype(BF)
    dpair = jnp.concatenate([(dhidden * up * slope).astype(BF), (dhidden * gelu).astype(BF)], axis=1)
    dpair_ref[...] = dpair
    part_a = dot(dpair, pair_a[...], NT)
    part_b = dot(dpair, pair_b[...], NT)

    @pl.when(step == 0)
    def _():
        second_sum[:, low] = part_a
        second_sum[:, high] = part_b

    @pl.when((step > 0) & (step < FF_TILES - 1))
    def _():
        second_sum[:, low] += part_a
        second_sum[:, high] += part_b

    @pl.when(step == FF_TILES - 1)
    def _():
        second_ref[:, low] = (second_sum[:, low] + part_a).astype(BF)
        second_ref[:, high] = (second_sum[:, high] + part_b).astype(BF)


def mlp(ring, blocks, cots, rest_mine, rest_other):
    whole = pl.BlockSpec((ROW, 1536), lambda f, r: (0, 0))
    table = pl.BlockSpec((RING, 1536), lambda f, r: (0, 0))
    half = pl.BlockSpec((RING, 768), lambda f, r: (0, 0))
    unit = pl.BlockSpec((RING, FF_TILE), lambda f, r: (0, f))
    pair_unit = pl.BlockSpec((RING, 2 * FF_TILE), lambda f, r: (0, f))
    pair = pl.BlockSpec((768, 2 * FF_TILE), lambda f, r: (0, 2 + f))
    down = pl.BlockSpec((768, FF_TILE), lambda f, r: (0, 10 + f))
    return call(
        mlp_kernel,
        "mlp",
        [((RING, FF), BF), ((RING, 2 * FF), BF), ((RING, 1536), BF), ((RING, 768), BF), ((RING, 1536), BF)],
        [ring, *blocks, cots, rest_mine, rest_other, rest_mine, rest_other],
        grid=(FF_TILES,),
        in_specs=[whole] * 4 + [table, pair, pair, down, down],
        out_specs=[unit, pair_unit, table, half, table],
        scratch=[pltpu.VMEM((RING, 1536), F32)],
        scalars=1,
    )


def down_project_kernel(ring_ref, hidden_ref, down_a, down_b, out_0, out_1, out_3, out_2, total):
    low, high = slice(0, 768), slice(768, 1536)
    total[:, low] = dot(hidden_ref[...], down_a[...], NT)
    total[:, high] = dot(hidden_ref[...], down_b[...], NT)
    for block, back in zip((out_0, out_1, out_3, out_2), BACKS):
        block[...] = total[ring_rows(ring_ref[0], back), :].astype(BF)


def down_project(ring, hidden, rest_mine, rest_other, needs):
    down = pl.BlockSpec((pl.Element(768), pl.Element(FF)), lambda f, r: (0, 1536 + 2 * FF))
    return call(
        down_project_kernel,
        "down_project",
        [((ROW, 1536), BF)] * 4,
        [ring, hidden, rest_mine, rest_other],
        needs=needs,
        grid=(1,),
        in_specs=[pl.BlockSpec((RING, FF), lambda f, r: (0, 0)), down, down],
        out_specs=[pl.BlockSpec((ROW, 1536), lambda f, r: (0, 0))] * 4,
        scratch=[pltpu.VMEM((RING, 1536), F32)],
        scalars=1,
    )


def out_grad_kernel(ring_ref, left_a, left_b, zero, one, three, two, mine_ref, other_ref, rights):
    for block, back in zip((zero, one, three, two), BACKS):
        rights[ring_rows(ring_ref[0], back), :] = block[...]
    mine_ref[...] = dot(left_a[...], rights[...], TN).astype(BF)
    other_ref[...] = dot(left_b[...], rights[...], TN).astype(BF)


def out_grad(ring, left, rights, needs=()):
    tile = 256
    steps = 768 // tile
    out = pl.BlockSpec((tile, 384), lambda i, r: (i, 0))
    return call(
        out_grad_kernel,
        "out_grad",
        [((768, 384), BF)] * 2,
        [ring, left, left, *rights],
        needs=needs,
        grid=(steps,),
        in_specs=[
            pl.BlockSpec((RING, tile), lambda i, r: (0, i)),
            pl.BlockSpec((RING, tile), lambda i, r: (0, i + steps)),
        ]
        + [pl.BlockSpec((ROW, 384), lambda i, r: (0, 0))] * 4,
        out_specs=[out, out],
        scratch=[pltpu.VMEM((RING, 384), BF)],
        scalars=1,
    )


def unit_grad_kernel(left, left_b, cot, cot_b, dpair, dpair_b, hidden, hidden_b, out_ref):
    pair = dot(left[...], dpair[...], TN) + dot(left_b[...], dpair_b[...], TN)
    down = dot(cot[...], hidden[...], TN) + dot(cot_b[...], hidden_b[...], TN)
    out_ref[:, : 2 * FF] = pair.astype(BF)
    out_ref[:, 2 * FF :] = down.astype(BF)


def unit_grad(args):
    tile = 256
    left = pl.BlockSpec((RING, tile), lambda i: (0, i))
    return call(
        unit_grad_kernel,
        "unit_grad",
        [((768, 3 * FF), BF)],
        args,
        micros=6.0,
        grid=(768 // tile,),
        in_specs=[left] * 4 + [pl.BlockSpec(a.shape, lambda i: (0, 0)) for a in args[4:]],
        out_specs=[pl.BlockSpec((tile, 3 * FF), lambda i: (i, 0))],
    )


def merge_kernel(mine_ref, other_ref, out_ref):
    out_ref[...] = (mine_ref[...].astype(F32) + other_ref[...].astype(F32)).astype(BF)


def merge(mine, other, needs=()):
    return call(merge_kernel, "merge", [(mine.shape, BF)], [mine, other], needs=needs)[0]


def normed(rows):
    values = rows.astype(F32)
    inverse = lax.rsqrt(jnp.mean(values * values, axis=-1, keepdims=True) + EPSILON)
    return values, values * inverse, inverse


def norm_back(grad, gain, n, inverse):
    scaled = grad * gain
    return inverse * (scaled - n * jnp.mean(scaled * n, axis=-1, keepdims=True))


def keyval_kernel(head_ref, own, one, three, mine_ref, other_ref, gain_ref, first_ref, keyval_ref):
    gain_ref[:, :768] = mine_ref[:, 640:].astype(F32).T[:8]
    gain_ref[:, 768:] = other_ref[:, 640:].astype(F32).T[:8]

    def project(block):
        first = (normed(block[...])[1] * gain_ref[0:1, :]).astype(BF)
        total = dot(first[:, :768], mine_ref[:, 384:640]) + dot(first[:, 768:], other_ref[:, 384:640])
        return first, total.astype(BF)

    first, total = project(own)
    first_ref[...] = first

    @pl.when(head_ref[0] == 0)
    def _():
        keyval_ref[:ROW, :] = total
        keyval_ref[ROW:, :] = project(three)[1]

    @pl.when(head_ref[0] == 1)
    def _():
        keyval_ref[:ROW, :] = project(one)[1]
        keyval_ref[ROW:, :] = total


def table_kernel(core_ref, mine_ref, other_ref, table_ref, last_ref):
    @pl.when(core_ref[0] == 0)
    def _():
        table_ref[: 2 * ROW, :] = mine_ref[...]
        table_ref[2 * ROW :, :] = other_ref[...]

    @pl.when(core_ref[0] == 1)
    def _():
        table_ref[: 2 * ROW, :] = other_ref[...]
        table_ref[2 * ROW :, :] = mine_ref[...]

    last_ref[...] = table_ref[512:, :]


def ring_cols(ring, ahead):
    return pl.ds(pl.multiple_of(lax.rem(ring + ahead, 4) * 384, 384), 384)


def turn_kernel(ring_ref, zero, one, two, three, out_ref):
    for ahead, block in enumerate((zero, one, two, three)):
        out_ref[:, ring_cols(ring_ref[0], ahead)] = block[...]


def split_kernel(ring_ref, rows_ref, zero, one, two, three):
    for ahead, block in enumerate((zero, one, two, three)):
        block[...] = rows_ref[:, ring_cols(ring_ref[0], ahead)]


def split(ring, rows):
    return call(split_kernel, "split", [((ROW, 384), BF)] * 4, [ring, rows], scalars=1)


def query_kernel(first_ref, one, three, two, gain_ref, mine_ref, other_ref, all_ref, *outs):
    all_ref[:ROW, :] = first_ref[...]
    for i, block in ((1, one), (2, three), (3, two)):
        all_ref[ROW * i : ROW * (i + 1), :] = (normed(block[...])[1] * gain_ref[0:1, :]).astype(BF)
    rows = all_ref[...]
    total = (dot(rows[:, :768], mine_ref[:, :384]) + dot(rows[:, 768:], other_ref[:, :384])).astype(BF)
    for i in range(4):
        outs[i][...] = total[ROW * i : ROW * (i + 1)]


def middle_kernel(attended_ref, mine_ref, other_ref, token_ref, gain_ref, middle_ref, second_ref):
    attended = attended_ref[...]
    branch = jnp.concatenate([dot(attended, mine_ref[...], NT), dot(attended, other_ref[...], NT)], axis=1)
    middle = token_ref[...].astype(F32) + branch
    middle_ref[...] = middle
    second_ref[...] = (normed(middle)[1] * gain_ref[1:2, :]).astype(BF)


def middle_back_kernel(
    parts, middle_ref, cot_ref, gain_ref, mine_ref, other_ref, grad_ref, low_ref, terms_ref, attended_ref
):
    grad_second = sum(parts[i].astype(F32) for i in range(4))
    _, n2, rs2 = normed(middle_ref[...])
    grad_middle = cot_ref[...].astype(F32) + norm_back(grad_second, gain_ref[1:2, :], n2, rs2)
    grad_ref[...] = grad_middle
    low = grad_middle.astype(BF)
    for i in range(4):
        low_ref[i] = low
    terms_ref[...] = (grad_second * n2).astype(BF)
    attended_ref[...] = (dot(low[:, :768], mine_ref[...]) + dot(low[:, 768:], other_ref[...])).astype(BF)


def first_back_kernel(
    dquery_0, dquery_1, dquery_3, dquery_2, home_6, home_5, home_4, home_3, home_2, home_1, home_0, rest_a, rest_b,
    first_ref, second_terms, own_ref, one, three, two, tail_a, tail_b, sums,
):
    dquery = jnp.concatenate([dquery_0[...], dquery_1[...], dquery_3[...], dquery_2[...]], axis=0)
    sums[...] = sum(home[...].astype(F32) for home in (home_5, home_4, home_3, home_2, home_1, home_0))
    sums[128:, :] += home_6[...].astype(F32)
    dkeyval = sums[...].astype(BF)
    column = lax.broadcasted_iota(jnp.int32, (RING + ROW, 128), 1)
    row = lax.broadcasted_iota(jnp.int32, (RING + ROW, 128), 0)
    picks = jnp.where(column == (row >= RING).astype(jnp.int32), 1.0, 0.0).astype(BF)
    for cols, rest, tail in ((slice(0, 768), rest_a, tail_a), (slice(768, 1536), rest_b, tail_b)):
        first = first_ref[:, cols]
        grads = dot(dquery, rest[:, :384], NT)
        own = grads[:ROW] + dot(dkeyval, rest[:, 384:640], NT)
        own_ref[:, cols] = own
        for i, ref in ((1, one), (2, three), (3, two)):
            ref[:, cols] = grads[ROW * i : ROW * (i + 1)].astype(BF)
        grads = jnp.concatenate([own, grads[ROW:]], axis=0)
        terms = jnp.concatenate([(grads * first.astype(F32)).astype(BF), second_terms[:, cols]], axis=0)
        tail[:, :384] = dot(first, dquery, TN).astype(BF)
        tail[:, 384:640] = dot(first[:ROW], dkeyval, TN).astype(BF)
        tail[:, 640:] = dot(terms, picks, TN).astype(BF)


def input_kernel(own_ref, one, three, two, token_ref, gain_ref, middle_ref, input_ref):
    grad_first = own_ref[...] + sum(part[...].astype(F32) for part in (one, three, two))
    _, n1, rs1 = normed(token_ref[...])
    input_ref[...] = (middle_ref[...] + norm_back(grad_first, gain_ref[0:1, :], n1, rs1)).astype(BF)


def shift_all(block, distance):
    count = 128
    route = [(i, i + distance) for i in range(count) if 0 <= i + distance < count]
    return lax.ppermute(block, AXES, route)


def shift_groups(block, distance):
    return lax.ppermute(block, ("z", "xh", "y"), [(i, i + distance) for i in range(32 - distance)])


def shift_x(block, distance):
    return lax.ppermute(block, CHIPS_X, [(i, (i + distance) % 4) for i in range(4)])


def swap(block, axis):
    return lax.ppermute(block, axis, [(0, 1), (1, 0)])


def shards(tokens, cotangent, w_query, w_key, w_value, w_out, w_gate, w_up, w_down, gain_attn, gain_mlp):
    core = lax.axis_index("core")
    xh = lax.axis_index("xh")
    head = lax.axis_index("head")
    ring = 2 * xh + head
    place = jnp.stack([lax.axis_index(AXES), 2 * core + head]).astype(jnp.int32)
    ring_scalar, core_scalar, head_scalar = (i.astype(jnp.int32).reshape(1) for i in (ring, core, head))
    eight = ("xh", "core", "head")
    four = ("xh", "core")

    def ordered(index, first, second, axis):
        return jnp.concatenate(
            [jnp.where(index == 0, first, second), jnp.where(index == 0, second, first)], axis=axis
        )

    def local_order(rows):
        cut = rows.reshape(ROW, 4, 2, 192)
        low = cut[:, :, 0].reshape(ROW, 768)
        high = cut[:, :, 1].reshape(ROW, 768)
        return ordered(core, low, high, 1)

    def true_order(rows):
        low = jnp.where(core == 0, rows[:, :768], rows[:, 768:]).reshape(ROW, 4, 192)
        high = jnp.where(core == 0, rows[:, 768:], rows[:, :768]).reshape(ROW, 4, 192)
        return jnp.stack([low, high], axis=2).reshape(ROW, 1536)

    def spread(piece):
        sent = jnp.broadcast_to(piece[None], (16,) + piece.shape)
        return lax.all_to_all(sent, PLANE, 0, 0, tiled=True).reshape(768, -1)

    def gather(piece):
        return lax.all_gather(piece, PLANE, axis=0, tiled=True)

    gains = jnp.pad(jnp.stack([gain_attn, gain_mlp], axis=1), ((0, 0), (0, 126)))
    query_cut = w_query.reshape(12, 2, 2, 384).transpose(2, 1, 0, 3)
    common = jnp.broadcast_to(jnp.concatenate([w_key, w_value, gains], axis=1), (2, 2, 12, 384))
    own_qkv = jnp.concatenate([query_cut, common], axis=3)
    own_attn = jnp.concatenate([jnp.broadcast_to(w_out.T, (2, 2, 24, 768)), own_qkv], axis=2)
    own_attn = jnp.broadcast_to(own_attn[:, None], (2, 2, 2, 36, 768)).reshape(8, 36, 768)
    got = lax.all_to_all(own_attn, eight, 0, 0, tiled=True)
    got = lax.dynamic_slice_in_dim(got, core * 4, 4, 0)
    qkv_piece = got[:, 24:].reshape(48, 768)
    out_piece = got[:, :24].reshape(2, 2, 24, 2, 384).transpose(0, 2, 3, 1, 4).reshape(48, 1536)
    token_own = local_order(tokens)
    token_1, token_3, token_2 = (local_order(shift_x(tokens, k)) for k in (1, 3, 2))
    qkv_mine = spread(qkv_piece)
    (qkv_mine,) = after([qkv_mine], token_1, token_3)

    pair_cut = jnp.stack([w_gate, w_up], axis=1).reshape(24, 2, 2, FF_TILES, FF_TILE)
    pair_cut = pair_cut.transpose(2, 0, 3, 1, 4).reshape(2, 24, 2 * FF)
    down_cut = w_down.T.reshape(24, 2, FF).transpose(1, 0, 2)
    own_mlp = jnp.concatenate([pair_cut, down_cut], axis=2)
    sent_a = jnp.where(core == 0, own_mlp[0], own_mlp[1])
    sent_b = jnp.where(core == 0, own_mlp[1], own_mlp[0])
    got_a = lax.ppermute(sent_a, four, [(0, 0), (1, 2), (2, 1), (3, 3)])
    got_b = lax.ppermute(sent_b, four, [(0, 2), (1, 0), (2, 3), (3, 1)])
    rest_mine = gather(jnp.concatenate([out_piece, ordered(xh, got_a, got_b, 0)], axis=1))

    qkv_other = swap(qkv_mine, "core")
    gain_rows, first_own, keyval_pair = call(
        keyval_kernel,
        "keyval",
        [((8, 1536), F32), ((ROW, 1536), BF), ((2 * ROW, 256), BF)],
        [head_scalar, token_own, token_1, token_3, qkv_mine, qkv_other],
        scalars=1,
    )
    here, last = call(
        table_kernel,
        "table",
        [((768, 256), BF), ((256, 256), BF)],
        [core_scalar, keyval_pair, swap(keyval_pair, "core")],
        scalars=1,
    )
    near, far = shift_groups(here, 1), shift_groups(last, 2)
    first_all, query_0, ring_1, ring_3, ring_2 = call(
        query_kernel,
        "query",
        [((RING, 1536), BF)] + [((ROW, 384), BF)] * 4,
        [first_own, token_1, token_3, token_2, gain_rows, qkv_mine, qkv_other],
        needs=[here],
    )
    query_1, query_3, query_2 = shift_x(ring_1, -1), shift_x(ring_3, -3), shift_x(ring_2, -2)
    (queries,) = call(
        turn_kernel, "turn", [((ROW, 1536), BF)], [ring_scalar, query_0, query_1, query_2, query_3], scalars=1
    )
    cot_own = local_order(cotangent)
    (cot_sent,) = after([cot_own], qkv_mine)
    cots = lax.all_to_all(jnp.broadcast_to(cot_sent[None], (4, ROW, 1536)), CHIPS_X, 0, 0, tiled=True)
    cots = cots.reshape(RING, 1536)
    attended, probs, keyval = attend(place, queries, far, near, here, [cots])

    attended_0, attended_1, attended_2, attended_3 = split(ring_scalar, attended)
    attended_1, attended_3, attended_2 = (
        shift_x(block, k) for block, k in ((attended_1, 1), (attended_3, 3), (attended_2, 2))
    )
    (rest_mine,) = after([rest_mine], attended)
    out_mine = rest_mine[:, :1536]
    out_other = swap(out_mine, "core")
    middle, second_own = call(
        middle_kernel,
        "middle",
        [((ROW, 1536), F32), ((ROW, 1536), BF)],
        [attended, out_mine, out_other, token_own, gain_rows],
    )
    blocks = [second_own] + [shift_x(second_own, k) for k in (1, 3, 2)]
    (rest_mine,) = after([rest_mine], out_other)
    rest_other = swap(rest_mine, "core")

    hidden, dpair, seconds, seconds_b, second_part = mlp(ring_scalar, blocks, cots, rest_mine, rest_other)
    second_home = lax.all_to_all(second_part.reshape(4, ROW, 1536), CHIPS_X, 0, 0, tiled=True)

    def planes(total):
        got = lax.all_to_all(total.reshape(16, 48, -1), PLANE, 0, 0, tiled=True)
        return jnp.sum(got.astype(F32), axis=0).astype(BF)

    (unit_total,) = unit_grad(
        [seconds, swap(seconds_b, "core"), cots, swap(cots[:, 768:], "core")]
        + [dpair, swap(dpair, "core"), hidden, swap(hidden, "core")]
    )
    (unit_total,) = after([unit_total], second_home)
    unit_grads = lax.psum_scatter(unit_total, PLANE, scatter_dimension=0, tiled=True)
    grad_middle, grad_branch, second_terms, grad_attended = call(
        middle_back_kernel,
        "middle_back",
        [((ROW, 1536), F32), ((4, ROW, 1536), BF), ((ROW, 1536), BF), ((ROW, 1536), BF)],
        [second_home, middle, cot_own, gain_rows, out_mine, out_other],
    )
    branches = lax.all_to_all(grad_branch, CHIPS_X, 0, 0, tiled=True).reshape(RING, 1536)
    dqueries, *homes = attend_back(queries, keyval, attended, grad_attended, probs, [])

    outs = down_project(ring_scalar, hidden, rest_mine, rest_other, [dqueries])
    dquery_0, dquery_1, dquery_2, dquery_3 = split(ring_scalar, dqueries)
    dquery_1, dquery_3, dquery_2 = (
        shift_x(block, k) for block, k in ((dquery_1, 1), (dquery_3, 3), (dquery_2, 2))
    )
    homes = [shift_all(home, -k) for home, k in zip(homes, (6, 5, 4, 3, 2, 1))] + [homes[6]]
    own_first, first_1, first_3, first_2, tail_mine, tail_other = call(
        first_back_kernel,
        "first_back",
        [((ROW, 1536), F32)] + [((ROW, 1536), BF)] * 3 + [((768, 768), BF)] * 2,
        [
            dquery_0, dquery_1, dquery_3, dquery_2, *homes, qkv_mine, qkv_other, first_all, second_terms,
        ],
        scratch=[pltpu.VMEM((ROW, 256), F32)],
    )
    tail_total = merge(tail_mine, swap(tail_other, "core"))
    tail_grads = planes(tail_total)
    mlp_own = outs[0].astype(F32)
    for out, k in zip(after(outs[1:], tail_mine), (1, 3, 2)):
        mlp_own = mlp_own + shift_x(out, -k).astype(F32)
    block_out = true_order((middle + mlp_own).astype(BF))
    tail_grads = tail_grads.reshape(4, 12, 768)
    tail_sent = jnp.where(jnp.arange(2).reshape(2, 1, 1, 1) == core, tail_grads[None], 0).reshape(8, 12, 768)
    tail_got = lax.all_to_all(tail_sent, eight, 0, 0, tiled=True).reshape(2, 2, 2, 12, 768)
    tail_got = jnp.where(xh == 0, tail_got[:, 0], tail_got[:, 1])
    grad_w_query = tail_got[..., :384].astype(F32).transpose(2, 1, 0, 3).reshape(12, 1536)
    tail_sum = jnp.sum(tail_got[..., 384:].astype(F32), axis=(0, 1))
    (input_grad,) = call(
        input_kernel,
        "input",
        [((ROW, 1536), BF)],
        [own_first, shift_x(first_1, -1), shift_x(first_3, -3), shift_x(first_2, -2), token_own, gain_rows, grad_middle],
        needs=[tail_got],
    )
    input_grad = true_order(input_grad)

    out_a, out_b = out_grad(
        ring_scalar, branches, [attended_0, attended_1, attended_3, attended_2], [tail_total]
    )
    out_grads = planes(merge(out_a, swap(out_b, "core"), needs=[tail_grads]))

    owned = jnp.concatenate([unit_grads, out_grads], axis=1)
    give_a = jnp.where(xh == 0, owned[:24], owned[24:])
    give_b = jnp.where(xh == 0, owned[24:], owned[:24])
    got_a = lax.ppermute(give_a, four, [(0, 0), (2, 1), (1, 2), (3, 3)])
    got_b = lax.ppermute(give_b, four, [(2, 0), (0, 1), (3, 2), (1, 3)])
    low = jnp.where(core == 0, got_a, got_b).astype(F32)
    high = jnp.where(core == 0, got_b, got_a).astype(F32)

    def both(start, width):
        return jnp.concatenate([low[:, start : start + width], high[:, start : start + width]], axis=1)

    def pair_out(which):
        cut = jnp.stack([low[:, : 2 * FF], high[:, : 2 * FF]], axis=1).reshape(24, 2, FF_TILES, 2, FF_TILE)
        return cut[:, :, :, which].reshape(24, 2 * FF)

    return (
        block_out,
        input_grad,
        grad_w_query,
        tail_sum[:, :128],
        tail_sum[:, 128:256],
        both(3 * FF, 384).T,
        pair_out(0),
        pair_out(1),
        both(2 * FF, FF).T,
        tail_sum[:, 256] / gain_attn.astype(F32),
        tail_sum[:, 257],
    )


def solution(mesh):
    grid = Mesh(mesh.devices.reshape(SIZES), AXES)
    seq = ("z", "xh", "y", "core")
    rows, both, cols = P(AXES, None), P(seq, "head"), P("head", seq)
    in_specs = (rows, rows, rows, rows, rows, cols, both, both, cols, P(AXES), P(AXES))
    out_specs = (rows, rows, rows, rows, rows, cols, both, both, cols, P(AXES), P(AXES))
    return jax.shard_map(shards, mesh=grid, in_specs=in_specs, out_specs=out_specs, check_vma=False)
```

time: 646 us -> 468 us (0.72)
  waiting for transfers between devices: 296 us -> 112 us
  Pallas kernels: 21 us -> 123 us
  matrix products: 83.2 us -> 0 us
  other arithmetic: 45.1 us -> 16.3 us
  local copies, waits for them, and re-layouts: 56 us -> 80.1 us
  blocking collectives: 10.3 us -> 0 us
    all_gather x3 -> x1, waiting for transfers between devices: 109 us -> 0.01 us  [gather(): return lax.all_gather(piece, PLANE, axis=0, tiled=True)]
    pallas_call x2 -> x24, Pallas kernels: 21 us -> 123 us  [the longest x18 123 us: call(): pl.pallas_call(body, out_shape=[jax.ShapeDtypeStruct(shape, kind) for sha...]
    dot_general x26 -> x0, matrix products: 83.2 us -> none  [dot(): return lax.dot_general(a, b, dims, preferred_element_type=F32)]
    all_to_all x10 -> x8, waiting for transfers between devices: 84.2 us -> 25.9 us  [the longest x1 9.89 us: shards(): got = lax.all_to_all(own_attn, eight, 0, 0, tiled=True)]
    ppermute x12 -> x6, waiting for transfers between devices: 48 us -> 6.65 us  [shift_all(): return lax.ppermute(block, AXES, route)]
    reduce_sum x11 -> x3, other arithmetic: 20.5 us -> 0.26 us  [the longest x2 0.25 us: planes(): return jnp.sum(got.astype(F32), axis=0).astype(BF)]
    ppermute x8 -> x16, waiting for transfers between devices: 0.02 us -> 18.6 us  [the longest x10 10 us: swap(): return lax.ppermute(block, axis, [(0, 1), (1, 0)])]
    ppermute x8 -> x16, starting transfers between devices: 1.1 us -> 18.7 us  [the longest x2 8.27 us: shift_groups(): lax.ppermute(block, ('z', 'xh', 'y'), [(i, i + distance) for i in range(3...]
  transfers between devices with their start and end apart: 45 -> 53, of which waited for: 24 -> 18; matrix products, arithmetic and copies ran while one was open for 25% -> 14% of each run, Pallas kernels for 3% -> 21%
where the time goes in v2:
time: 468 us; the launch traced here: 460 us
  Pallas kernels  123 us (26%)
  starting transfers between devices  113 us (24%)
  waiting for transfers between devices  112 us (24%)
  local copies, waits for them, and re-layouts  80.1 us (17%)
  other arithmetic  16.3 us (3%)
  between operations  15.4 us (3%)
    pallas_call x18, Pallas kernels, call(): pl.pallas_call(body, out_shape=[jax.ShapeDtypeStruct(shape, kind) for sha...  123 us
    ppermute x21, waiting for transfers between devices, shift_x(): lax.ppermute(block, CHIPS_X, [(i, (i + distance) % 4) for i in range(4)])  60.9 us
    ppermute x21, starting transfers between devices, shift_x(): lax.ppermute(block, CHIPS_X, [(i, (i + distance) % 4) for i in range(4)])  28.4 us
    ppermute x6, starting transfers between devices, shift_all(): return lax.ppermute(block, AXES, route)  25.6 us
    unnamed x113, local copies, waits for them, and re-layouts  23.2 us
    all_to_all x2, starting transfers between devices, planes(): got = lax.all_to_all(total.reshape(16, 48, -1), PLANE, 0, 0, tiled=True)  12.7 us
    reshape x5, local copies, waits for them, and re-layouts, local_order(): cut = rows.reshape(ROW, 4, 2, 192)  10.5 us
    ppermute x10, waiting for transfers between devices, swap(): return lax.ppermute(block, axis, [(0, 1), (1, 0)])  10 us
  transfers between devices with their start and end apart: 53, of which 18 were waited for; matrix products, arithmetic and copies ran while one was open for 14% of the time, Pallas kernels for 21%

profile of v2, /device:TPU:64, one launch (start us, length us, event | category | flops | bytes accessed | tf_op | source)
XLA Modules:
  0.0 460.2 jit_solution(11205105922441784405)
XLA Ops:
  11.5 4.4 collective-permute-start.11
  17.0 4.2 all-to-all-start
  21.3 9.9 %all-to-all-done = bf16[8,36,768]{2,1,0:T(8,128)(2,1)S(1)} async-done(((bf16[8,36,768]{2,1,0:T(8,128)(2,1)}), bf16[8,36,768]{2,1,0:T(8,128)(2,1)S(1)}, u32[]{:S(2)}, u32[]{:S(2)}) %all-to-all-start) | async-done | bytes 442400 | tf_op jit(solution)/shard_map/all_to_all | solution.py:533
  39.0 7.9 %all-to-all-start.1 = ((bf16[16,48,768]{2,1,0:T(8,128)(2,1)}), bf16[16,48,768]{2,1,0:T(8,128)(2,1)S(1)}, u32[]{:S(2)}, u32[]{:S(2)}) async-start(bf16[16,48,768]{2,1,0:T(8,128)(2,1)} %broadcast_in_dim.57), calls=%async_computation.1 | async-start | bytes 2359296 | tf_op jit(solution)/shard_map/all_to_all | solution.py:522
  49.6 12.8 %collective-permute-done = bf16[192,1536]{1,0:T(8,128)(2,1)} collective-permute-done((bf16[192,1536]{1,0:T(8,128)(2,1)}, bf16[192,1536]{1,0:T(8,128)(2,1)}, u32[]{:S(2)}, u32[]{:S(2)}) %collective-permute-start) | collective-permute-done | bytes 589856 | tf_op jit(solution)/shard_map/ppermute | solution.py:487
  110.0 4.0 keyval.1
  124.0 5.3 %query.1 = (bf16[768,1536]{1,0:T(8,128)(2,1)}, bf16[192,384]{1,0:T(8,128)(2,1)}, bf16[192,384]{1,0:T(8,128)(2,1)}, bf16[192,384]{1,0:T(8,128)(2,1)}, bf16[192,384]{1,0:T(8,128)(2,1)}) custom-call(bf16[192,1536]{1,0:T(8,128)(2,1)} %get-tuple-element.66.refs_0_, bf16[192,1536]{1,0:T(8,128)(2,1)} %copy-done.9, bf16[192,1536]{1,0:T(8,128)(2,1)} %copy-done.8, ...), custom_call_target="tpu_custom_call" | custom-call | flops 10000000 | bytes 1000000 | tf_op jit(solution)/shard_map/query/pallas_call | solution.py:70
  134.0 4.8 %collective-permute-start.8 = (bf16[256,256]{1,0:T(8,128)(2,1)S(1)}, bf16[256,256]{1,0:T(8,128)(2,1)S(1)}, u32[]{:S(2)}, u32[]{:S(2)}) collective-permute-start(bf16[256,256]{1,0:T(8,128)(2,1)S(1)} %copy-done.50), channel_id=1, source_target_pairs={{0,8},{4,12},{8,16},{12,20},{16,24},{20,28},{24,32},{28,36},{32,40... | collective-permute-start | bytes 393224 | tf_op jit(solution)/shard_map/ppermute | solution.py:483
  148.9 11.2 %attend.1 = (bf16[192,1536]{1,0:T(8,128)(2,1)}, bf16[6,1216,384]{2,1,0:T(8,128)(2,1)}, bf16[1216,256]{1,0:T(8,128)(2,1)}) custom-call(s32[2]{0:T(128)} %pad_add_fusion.refs_0_, bf16[192,1536]{1,0:T(8,128)(2,1)} %turn.1.refs_1_.refs_0_, bf16[256,256]{1,0:T(8,128)(2,1)} %copy-done.38, bf16[768,256]{1,0:T(8,128)(2,1)} %copy-done.28, ...), custom_call_target="tpu_custom_call" | custom-call | flops 10000000 | bytes 1000000 | tf_op jit(solution)/shard_map/attend/pallas_call | solution.py:70
  163.3 4.5 collective-permute-done.12.refs_2_.refs_1_.refs_5_
  169.8 5.6 %middle.1 = (f32[192,1536]{1,0:T(8,128)}, bf16[192,1536]{1,0:T(8,128)(2,1)}) custom-call(bf16[192,1536]{1,0:T(8,128)(2,1)} %get-tuple-element.75.refs_1_.refs_0_.refs_2_, bf16[768,1536]{1,0:T(8,128)(2,1)} %copy-done.6, bf16[768,1536]{1,0:T(8,128)(2,1)} %copy-done.5, bf16[192,1536]{1,0:T(8,128)(2,1)} %copy-done.10, ...), custom_call_target="tpu_custom_call" | custom-call | flops 10000000 | bytes 1000000 | tf_op jit(solution)/shard_map/middle/pallas_call | solution.py:70
  178.8 26.3 %collective-permute-done.13.refs_2_ = bf16[192,1536]{1,0:T(8,128)(2,1)S(1)} collective-permute-done((bf16[192,1536]{1,0:T(8,128)(2,1)}, bf16[192,1536]{1,0:T(8,128)(2,1)S(1)}, u32[]{:S(2)}, u32[]{:S(2)}) %collective-permute-start.13) | collective-permute-done | bytes 589856 | tf_op jit(solution)/shard_map/ppermute | solution.py:487
  209.9 26.6 %mlp.1 = (bf16[768,1152]{1,0:T(8,128)(2,1)}, bf16[768,2304]{1,0:T(8,128)(2,1)}, bf16[768,1536]{1,0:T(8,128)(2,1)}, bf16[768,768]{1,0:T(8,128)(2,1)}, bf16[768,1536]{1,0:T(8,128)(2,1)}) custom-call(s32[1]{0:T(128)} %bitcast.2.refs_0_, bf16[192,1536]{1,0:T(8,128)(2,1)} %get-tuple-element.77.refs_1_, bf16[192,1536]{1,0:T(8,128)(2,1)} %copy-done.25, ...), custom_call_target="tpu_custom_call" | custom-call | flops 10000000 | bytes 1000000 | tf_op jit(solution)/shard_map/mlp/pallas_call | solution.py:70
  237.1 4.6 %all-to-all-start.3 = ((bf16[4,192,1536]{2,1,0:T(8,128)(2,1)}), bf16[4,192,1536]{2,1,0:T(8,128)(2,1)}, u32[]{:S(2)}, u32[]{:S(2)}) async-start(bf16[4,192,1536]{2,1,0:T(8,128)(2,1)} %bitcast.86), calls=%async_computation.3 | async-start | bytes 4718592 | tf_op jit(solution)/shard_map/all_to_all | solution.py:603
  249.8 15.2 %unit_grad.1.refs_0_ = bf16[768,3456]{1,0:T(8,128)(2,1)} custom-call(bf16[768,1536]{1,0:T(8,128)(2,1)} %get-tuple-element.111.refs_0_, bf16[768,768]{1,0:T(8,128)(2,1)} %copy-done.14, bf16[768,1536]{1,0:T(8,128)(2,1)} %bitcast.79, bf16[768,768]{1,0:T(8,128)(2,1)} %copy-done.13, bf16[768,2304]{1,0:T(8,128)(2,1)} %get-tuple-element.113.refs_4_, ...), custom_call_target="tpu_custom_call" | custom-call | flops 6000000000 | bytes 1000000 | tf_op jit(solution)/shard_map/unit_grad/pallas_call | solution.py:70
  265.0 6.5 %all-to-all-done.3.refs_0_.refs_1_ = bf16[4,192,1536]{2,1,0:T(8,128)(2,1)} async-done(((bf16[4,192,1536]{2,1,0:T(8,128)(2,1)}), bf16[4,192,1536]{2,1,0:T(8,128)(2,1)}, u32[]{:S(2)}, u32[]{:S(2)}) %all-to-all-start.3) | async-done | bytes 2359328 | tf_op jit(solution)/shard_map/all_to_all | solution.py:603
  271.5 6.8 %middle_back.1 = (f32[192,1536]{1,0:T(8,128)}, bf16[4,192,1536]{2,1,0:T(8,128)(2,1)}, bf16[192,1536]{1,0:T(8,128)(2,1)}, bf16[192,1536]{1,0:T(8,128)(2,1)}) custom-call(bf16[4,192,1536]{2,1,0:T(8,128)(2,1)} %all-to-all-done.3.refs_0_.refs_1_, f32[192,1536]{1,0:T(8,128)} %get-tuple-element.76.refs_1_, ...), custom_call_target="tpu_custom_call" | custom-call | flops 10000000 | bytes 1000000 | tf_op jit(solution)/shard_map/middle_back/pallas_call | solution.py:70
  282.0 10.5 %attend_back.1 = (bf16[192,1536]{1,0:T(8,128)(2,1)}, bf16[64,256]{1,0:T(8,128)(2,1)}, bf16[192,256]{1,0:T(8,128)(2,1)}, bf16[192,256]{1,0:T(8,128)(2,1)}, bf16[1...) custom-call(bf16[192,1536]{1,0:T(8,128)(2,1)} %turn.1.refs_1_.refs_0_, ...), custom_call_target="tpu_custom_call" | custom-call | flops 6000000000 | bytes 1000000 | tf_op jit(solution)/shard_map/attend_back/pallas_call | solution.py:70
  292.4 4.8 %collective-permute-start.21 = (bf16[192,256]{1,0:T(8,128)(2,1)}, bf16[192,256]{1,0:T(8,128)(2,1)S(1)}, u32[]{:S(2)}, u32[]{:S(2)}) collective-permute-start(bf16[192,256]{1,0:T(8,128)(2,1)} %get-tuple-element.93), channel_id=1, source_target_pairs={{5,0},{6,1},{7,2},{8,3},{9,4},{10,5},{11,6},{12,7},{13,8},{14,9},{... | collective-permute-start | bytes 294920 | tf_op jit(solution)/shard_map/ppermute | solution.py:479
  297.3 5.2 %collective-permute-start.22 = (bf16[192,256]{1,0:T(8,128)(2,1)}, bf16[192,256]{1,0:T(8,128)(2,1)S(1)}, u32[]{:S(2)}, u32[]{:S(2)}) collective-permute-start(bf16[192,256]{1,0:T(8,128)(2,1)} %get-tuple-element.94), channel_id=1, source_target_pairs={{4,0},{5,1},{6,2},{7,3},{8,4},{9,5},{10,6},{11,7},{12,8},{13,9},{1... | collective-permute-start | bytes 294920 | tf_op jit(solution)/shard_map/ppermute | solution.py:479
  316.9 8.9 %collective-permute-start.24 = (bf16[192,256]{1,0:T(8,128)(2,1)}, bf16[192,256]{1,0:T(8,128)(2,1)S(1)}, u32[]{:S(2)}, u32[]{:S(2)}) collective-permute-start(bf16[192,256]{1,0:T(8,128)(2,1)} %get-tuple-element.96), channel_id=1, source_target_pairs={{2,0},{3,1},{4,2},{5,3},{6,4},{7,5},{8,6},{9,7},{10,8},{11,9},{12,... | collective-permute-start | bytes 294920 | tf_op jit(solution)/shard_map/ppermute | solution.py:479
  333.3 8.3 %first_back.1 = (f32[192,1536]{1,0:T(8,128)}, bf16[192,1536]{1,0:T(8,128)(2,1)}, bf16[192,1536]{1,0:T(8,128)(2,1)}, bf16[192,1536]{1,0:T(8,128)(2,1)}, bf16[768,...) custom-call(bf16[192,384]{1,0:T(8,128)(2,1)} %get-tuple-element.88.refs_0_, bf16[192,384]{1,0:T(8,128)(2,1)} %copy-done.30, ...), custom_call_target="tpu_custom_call" | custom-call | flops 10000000 | bytes 1000000 | tf_op jit(solution)/shard_map/first_back/pallas_call | solution.py:70
  341.8 7.9 %down_project.1 = (bf16[192,1536]{1,0:T(8,128)(2,1)}, bf16[192,1536]{1,0:T(8,128)(2,1)}, bf16[192,1536]{1,0:T(8,128)(2,1)}, bf16[192,1536]{1,0:T(8,128)(2,1)}) custom-call(s32[1]{0:T(128)} %bitcast.2.refs_0_, bf16[768,1152]{1,0:T(8,128)(2,1)} %get-tuple-element.78.refs_1_.refs_6_, bf16[768,4992]{1,0:T(8,128)(2,1)} %after.9.refs_6_.refs_8_.refs_2_, ...), custom_call_target="tpu_custom_call" | custom-call | flops 10000000 | bytes 1000000 | tf_op jit(solution)/shard_map/down_project/pallas_call | solution.py:70
  361.7 7.4 %all-to-all-start.4 = ((bf16[16,48,768]{2,1,0:T(8,128)(2,1)}), bf16[16,48,768]{2,1,0:T(8,128)(2,1)S(1)}, u32[]{:S(2)}, u32[]{:S(2)}) async-start(bf16[16,48,768]{2,1,0:T(8,128)(2,1)} %bitcast.84), calls=%async_computation.4 | async-start | bytes 2359296 | tf_op jit(solution)/shard_map/all_to_all | solution.py:606
  370.8 12.1 %collective-permute-done.37.refs_4_ = bf16[192,384]{1,0:T(8,128)(2,1)} collective-permute-done((bf16[192,384]{1,0:T(8,128)(2,1)}, bf16[192,384]{1,0:T(8,128)(2,1)}, u32[]{:S(2)}, u32[]{:S(2)}) %collective-permute-start.37) | collective-permute-done | bytes 147488 | tf_op jit(solution)/shard_map/ppermute | solution.py:487
  386.0 4.4 collective-permute-done.39.refs_6_
  391.6 4.7 %out_grad.1 = (bf16[768,384]{1,0:T(8,128)(2,1)}, bf16[768,384]{1,0:T(8,128)(2,1)}) custom-call(s32[1]{0:T(128)} %bitcast.2.refs_0_, bf16[768,1536]{1,0:T(8,128)(2,1)} %bitcast.82, bf16[768,1536]{1,0:T(8,128)(2,1)} %bitcast.83, bf16[192,384]{1,0:T(8,128)(2,1)} %get-tuple-element.115.refs_3_, bf16[192,384]{1,0:T(8,128)(2,1)} %collective-permute-done.37.refs_4_, ...), custom_call_target="tpu_custom_call" | custom-call | flops 10000000 | bytes 1000000 | tf_op jit(solution)/shard_map/out_grad/pallas_call | solution.py:70
  401.1 3.8 all-to-all-start.5
  411.2 9.5 %all-to-all-done.5 = bf16[8,12,768]{2,1,0:T(8,128)(2,1)S(1)} async-done(((bf16[8,12,768]{2,1,0:T(8,128)(2,1)}), bf16[8,12,768]{2,1,0:T(8,128)(2,1)S(1)}, u32[]{:S(2)}, u32[]{:S(2)}) %all-to-all-start.5) | async-done | bytes 147488 | tf_op jit(solution)/shard_map/all_to_all | solution.py:647
  420.8 5.3 %all-to-all-start.7 = ((bf16[16,48,384]{2,1,0:T(8,128)(2,1)}), bf16[16,48,384]{2,1,0:T(8,128)(2,1)S(1)}, u32[]{:S(2)}, u32[]{:S(2)}) async-start(bf16[16,48,384]{2,1,0:T(8,128)(2,1)} %bitcast.85), calls=%async_computation.7 | async-start | bytes 1179648 | tf_op jit(solution)/shard_map/all_to_all | solution.py:606
  426.7 4.1 input.1
  442.9 6.6 %collective-permute-done.42 = bf16[24,3840]{1,0:T(8,128)(2,1)S(1)} collective-permute-done((bf16[24,3840]{1,0:T(8,128)(2,1)S(1)}, bf16[24,3840]{1,0:T(8,128)(2,1)S(1)}, u32[]{:S(2)}, u32[]{:S(2)}) %collective-permute-start.42) | collective-permute-done | bytes 184352 | tf_op jit(solution)/shard_map/ppermute | solution.py:669
  (314 shorter events, 180.7 us)
Async XLA Ops:
  21.2 138.8 %all-gather.2.cloned.1.call-start = ((), (), s32[]{:S(2)}) async-start(), calls=%async_computation.9 | async-start | bytes 8146944 | tf_op jit(solution)/shard_map/all_gather | solution.py:525
  32.4 16.5 %collective-permute-start.1 = (bf16[192,1536]{1,0:T(8,128)(2,1)}, bf16[192,1536]{1,0:T(8,128)(2,1)S(1)}, u32[]{:S(2)}, u32[]{:S(2)}) collective-permute-start(bf16[192,1536]{1,0:T(8,128)(2,1)} %param.11), channel_id=1, source_target_pairs={{0,17},{1,0},{16,1},{17,16},{2,19},{3,2},{18,3},{19,18},{4,21},{5,... | collective-permute-start | bytes 1769480 | tf_op jit(solution)/shard_map/ppermute | solution.py:487
  33.6 28.8 %collective-permute-start = (bf16[192,1536]{1,0:T(8,128)(2,1)}, bf16[192,1536]{1,0:T(8,128)(2,1)}, u32[]{:S(2)}, u32[]{:S(2)}) collective-permute-start(bf16[192,1536]{1,0:T(8,128)(2,1)} %param.11), channel_id=1, source_target_pairs={{0,1},{1,16},{16,17},{17,0},{2,3},{3,18},{18,19},{19,2},{4,5},{5,2... | collective-permute-start | bytes 1769480 | tf_op jit(solution)/shard_map/ppermute | solution.py:487
  34.5 40.9 %collective-permute-start.3 = (bf16[192,1536]{1,0:T(8,128)(2,1)}, bf16[192,1536]{1,0:T(8,128)(2,1)}, u32[]{:S(2)}, u32[]{:S(2)}) collective-permute-start(bf16[192,1536]{1,0:T(8,128)(2,1)} %param.11), channel_id=1, source_target_pairs={{0,16},{1,17},{16,0},{17,1},{2,18},{3,19},{18,2},{19,3},{4,20},{5,... | collective-permute-start | bytes 1769480 | tf_op jit(solution)/shard_map/ppermute | solution.py:487
  39.0 44.5 %all-to-all-start.1 = ((bf16[16,48,768]{2,1,0:T(8,128)(2,1)}), bf16[16,48,768]{2,1,0:T(8,128)(2,1)S(1)}, u32[]{:S(2)}, u32[]{:S(2)}) async-start(bf16[16,48,768]{2,1,0:T(8,128)(2,1)} %broadcast_in_dim.57), calls=%async_computation.1 | async-start | bytes 2359296 | tf_op jit(solution)/shard_map/all_to_all | solution.py:522
  84.9 23.9 %collective-permute-start.2 = (bf16[768,768]{1,0:T(8,128)(2,1)}, bf16[768,768]{1,0:T(8,128)(2,1)S(1)}, u32[]{:S(2)}, u32[]{:S(2)}) collective-permute-start(bf16[768,768]{1,0:T(8,128)(2,1)} %after.6.refs_4_.refs_5_.refs_1_.refs_11_), channel_id=1, source_target_pairs={{0,2},{2,0},{1,3},{3,1},{4,6},{6,4},{5,7},{7,5},{8,10},{10,8},{9,1... | collective-permute-start | bytes 3538952 | tf_op jit(solution)/shard_map/ppermute | solution.py:491
  91.4 55.9 %all-to-all-start.2 = ((bf16[4,192,1536]{2,1,0:T(8,128)(2,1)}), bf16[4,192,1536]{2,1,0:T(8,128)(2,1)S(1)}, u32[]{:S(2)}, u32[]{:S(2)}) async-start(bf16[4,192,1536]{2,1,0:T(8,128)(2,1)} %broadcast_in_dim.58), calls=%async_computation.2 | async-start | bytes 4718592 | tf_op jit(solution)/shard_map/all_to_all | solution.py:581
  119.7 27.6 %collective-permute-start.9 = (bf16[768,256]{1,0:T(8,128)(2,1)}, bf16[768,256]{1,0:T(8,128)(2,1)S(1)}, u32[]{:S(2)}, u32[]{:S(2)}) collective-permute-start(bf16[768,256]{1,0:T(8,128)(2,1)} %get-tuple-element.69.refs_7_.refs_4_), channel_id=1, source_target_pairs={{0,4},{4,8},{8,12},{12,16},{16,20},{20,24},{24,28},{28,32},{32,36}... | collective-permute-start | bytes 1179656 | tf_op jit(solution)/shard_map/ppermute | solution.py:483
  169.3 37.5 %collective-permute-start.16 = (bf16[768,4992]{1,0:T(8,128)(2,1)}, bf16[768,4992]{1,0:T(8,128)(2,1)S(1)}, u32[]{:S(2)}, u32[]{:S(2)}) collective-permute-start(bf16[768,4992]{1,0:T(8,128)(2,1)} %after.9.refs_6_.refs_8_.refs_2_), channel_id=1, source_target_pairs={{0,2},{2,0},{1,3},{3,1},{4,6},{6,4},{5,7},{7,5},{8,10},{10,8},{9,1... | collective-permute-start | bytes 23003144 | tf_op jit(solution)/shard_map/ppermute | solution.py:491
  175.4 29.7 %collective-permute-start.13 = (bf16[192,1536]{1,0:T(8,128)(2,1)}, bf16[192,1536]{1,0:T(8,128)(2,1)S(1)}, u32[]{:S(2)}, u32[]{:S(2)}) collective-permute-start(bf16[192,1536]{1,0:T(8,128)(2,1)} %get-tuple-element.77.refs_1_), channel_id=1, source_target_pairs={{0,1},{1,16},{16,17},{17,0},{2,3},{3,18},{18,19},{19,2},{4,5},{5,2... | collective-permute-start | bytes 1769480 | tf_op jit(solution)/shard_map/ppermute | solution.py:487
  175.6 29.5 %collective-permute-start.14 = (bf16[192,1536]{1,0:T(8,128)(2,1)}, bf16[192,1536]{1,0:T(8,128)(2,1)S(1)}, u32[]{:S(2)}, u32[]{:S(2)}) collective-permute-start(bf16[192,1536]{1,0:T(8,128)(2,1)} %get-tuple-element.77.refs_1_), channel_id=1, source_target_pairs={{0,17},{1,0},{16,1},{17,16},{2,19},{3,2},{18,3},{19,18},{4,21},{5,... | collective-permute-start | bytes 1769480 | tf_op jit(solution)/shard_map/ppermute | solution.py:487
  178.7 27.3 %collective-permute-start.15 = (bf16[192,1536]{1,0:T(8,128)(2,1)}, bf16[192,1536]{1,0:T(8,128)(2,1)S(1)}, u32[]{:S(2)}, u32[]{:S(2)}) collective-permute-start(bf16[192,1536]{1,0:T(8,128)(2,1)} %get-tuple-element.77.refs_1_), channel_id=1, source_target_pairs={{0,16},{1,17},{16,0},{17,1},{2,18},{3,19},{18,2},{19,3},{4,20},{5,... | collective-permute-start | bytes 1769480 | tf_op jit(solution)/shard_map/ppermute | solution.py:487
  237.1 34.4 %all-to-all-start.3 = ((bf16[4,192,1536]{2,1,0:T(8,128)(2,1)}), bf16[4,192,1536]{2,1,0:T(8,128)(2,1)}, u32[]{:S(2)}, u32[]{:S(2)}) async-start(bf16[4,192,1536]{2,1,0:T(8,128)(2,1)} %bitcast.86), calls=%async_computation.3 | async-start | bytes 4718592 | tf_op jit(solution)/shard_map/all_to_all | solution.py:603
  241.7 196.4 %reduce-scatter.4.cloned.1.call-start = ((), (), s32[]{:S(2)}) async-start(), calls=%async_computation.10 | async-start | bytes 5640192
  278.3 82.0 %all-to-all-start.6 = ((bf16[4,192,1536]{2,1,0:T(8,128)(2,1)}), bf16[4,192,1536]{2,1,0:T(8,128)(2,1)S(1)}, u32[]{:S(2)}, u32[]{:S(2)}) async-start(bf16[4,192,1536]{2,1,0:T(8,128)(2,1)} %get-tuple-element.114), calls=%async_computation.6 | async-start | bytes 4718592 | tf_op jit(solution)/shard_map/all_to_all | solution.py:621
  292.4 21.8 %collective-permute-start.21 = (bf16[192,256]{1,0:T(8,128)(2,1)}, bf16[192,256]{1,0:T(8,128)(2,1)S(1)}, u32[]{:S(2)}, u32[]{:S(2)}) collective-permute-start(bf16[192,256]{1,0:T(8,128)(2,1)} %get-tuple-element.93), channel_id=1, source_target_pairs={{5,0},{6,1},{7,2},{8,3},{9,4},{10,5},{11,6},{12,7},{13,8},{14,9},{... | collective-permute-start | bytes 294920 | tf_op jit(solution)/shard_map/ppermute | solution.py:479
  297.3 19.6 %collective-permute-start.22 = (bf16[192,256]{1,0:T(8,128)(2,1)}, bf16[192,256]{1,0:T(8,128)(2,1)S(1)}, u32[]{:S(2)}, u32[]{:S(2)}) collective-permute-start(bf16[192,256]{1,0:T(8,128)(2,1)} %get-tuple-element.94), channel_id=1, source_target_pairs={{4,0},{5,1},{6,2},{7,3},{8,4},{9,5},{10,6},{11,7},{12,8},{13,9},{1... | collective-permute-start | bytes 294920 | tf_op jit(solution)/shard_map/ppermute | solution.py:479
  302.5 23.2 %collective-permute-start.23 = (bf16[192,256]{1,0:T(8,128)(2,1)}, bf16[192,256]{1,0:T(8,128)(2,1)S(1)}, u32[]{:S(2)}, u32[]{:S(2)}) collective-permute-start(bf16[192,256]{1,0:T(8,128)(2,1)} %get-tuple-element.95), channel_id=1, source_target_pairs={{3,0},{4,1},{5,2},{6,3},{7,4},{8,5},{9,6},{10,7},{11,8},{12,9},{13... | collective-permute-start | bytes 294920 | tf_op jit(solution)/shard_map/ppermute | solution.py:479
  309.2 23.3 %collective-permute-start.17 = (bf16[192,384]{1,0:T(8,128)(2,1)}, bf16[192,384]{1,0:T(8,128)(2,1)S(1)}, u32[]{:S(2)}, u32[]{:S(2)}) collective-permute-start(bf16[192,384]{1,0:T(8,128)(2,1)} %get-tuple-element.89), channel_id=1, source_target_pairs={{0,1},{1,16},{16,17},{17,0},{2,3},{3,18},{18,19},{19,2},{4,5},{5,2... | collective-permute-start | bytes 442376 | tf_op jit(solution)/shard_map/ppermute | solution.py:487
  311.5 21.0 %collective-permute-start.18 = (bf16[192,384]{1,0:T(8,128)(2,1)}, bf16[192,384]{1,0:T(8,128)(2,1)S(1)}, u32[]{:S(2)}, u32[]{:S(2)}) collective-permute-start(bf16[192,384]{1,0:T(8,128)(2,1)} %get-tuple-element.90), channel_id=1, source_target_pairs={{0,17},{1,0},{16,1},{17,16},{2,19},{3,2},{18,3},{19,18},{4,21},{5,... | collective-permute-start | bytes 442376 | tf_op jit(solution)/shard_map/ppermute | solution.py:487
  314.3 18.2 %collective-permute-start.19 = (bf16[192,384]{1,0:T(8,128)(2,1)}, bf16[192,384]{1,0:T(8,128)(2,1)S(1)}, u32[]{:S(2)}, u32[]{:S(2)}) collective-permute-start(bf16[192,384]{1,0:T(8,128)(2,1)} %get-tuple-element.91), channel_id=1, source_target_pairs={{0,16},{1,17},{16,0},{17,1},{2,18},{3,19},{18,2},{19,3},{4,20},{5,... | collective-permute-start | bytes 442376 | tf_op jit(solution)/shard_map/ppermute | solution.py:487
  349.6 46.7 %collective-permute-start.28 = (bf16[192,1536]{1,0:T(8,128)(2,1)}, bf16[192,1536]{1,0:T(8,128)(2,1)}, u32[]{:S(2)}, u32[]{:S(2)}) collective-permute-start(bf16[192,1536]{1,0:T(8,128)(2,1)} %get-tuple-element.104), channel_id=1, source_target_pairs={{0,16},{1,17},{16,0},{17,1},{2,18},{3,19},{18,2},{19,3},{4,20},{5,... | collective-permute-start | bytes 1769480 | tf_op jit(solution)/shard_map/ppermute | solution.py:487
  351.2 46.3 %collective-permute-start.27 = (bf16[192,1536]{1,0:T(8,128)(2,1)}, bf16[192,1536]{1,0:T(8,128)(2,1)}, u32[]{:S(2)}, u32[]{:S(2)}) collective-permute-start(bf16[192,1536]{1,0:T(8,128)(2,1)} %get-tuple-element.103), channel_id=1, source_target_pairs={{0,1},{1,16},{16,17},{17,0},{2,3},{3,18},{18,19},{19,2},{4,5},{5,2... | collective-permute-start | bytes 1769480 | tf_op jit(solution)/shard_map/ppermute | solution.py:487
  351.2 46.4 %collective-permute-start.26 = (bf16[192,1536]{1,0:T(8,128)(2,1)}, bf16[192,1536]{1,0:T(8,128)(2,1)}, u32[]{:S(2)}, u32[]{:S(2)}) collective-permute-start(bf16[192,1536]{1,0:T(8,128)(2,1)} %get-tuple-element.102), channel_id=1, source_target_pairs={{0,17},{1,0},{16,1},{17,16},{2,19},{3,2},{18,3},{19,18},{4,21},{5,... | collective-permute-start | bytes 1769480 | tf_op jit(solution)/shard_map/ppermute | solution.py:487
  356.4 26.5 %collective-permute-start.37 = (bf16[192,384]{1,0:T(8,128)(2,1)}, bf16[192,384]{1,0:T(8,128)(2,1)}, u32[]{:S(2)}, u32[]{:S(2)}) collective-permute-start(bf16[192,384]{1,0:T(8,128)(2,1)} %get-tuple-element.116), channel_id=1, source_target_pairs={{0,1},{1,16},{16,17},{17,0},{2,3},{3,18},{18,19},{19,2},{4,5},{5,2... | collective-permute-start | bytes 442376 | tf_op jit(solution)/shard_map/ppermute | solution.py:487
  361.7 38.4 %all-to-all-start.4 = ((bf16[16,48,768]{2,1,0:T(8,128)(2,1)}), bf16[16,48,768]{2,1,0:T(8,128)(2,1)S(1)}, u32[]{:S(2)}, u32[]{:S(2)}) async-start(bf16[16,48,768]{2,1,0:T(8,128)(2,1)} %bitcast.84), calls=%async_computation.4 | async-start | bytes 2359296 | tf_op jit(solution)/shard_map/all_to_all | solution.py:606
  369.1 15.6 %collective-permute-start.38 = (bf16[192,384]{1,0:T(8,128)(2,1)}, bf16[192,384]{1,0:T(8,128)(2,1)S(1)}, u32[]{:S(2)}, u32[]{:S(2)}) collective-permute-start(bf16[192,384]{1,0:T(8,128)(2,1)} %get-tuple-element.117), channel_id=1, source_target_pairs={{0,17},{1,0},{16,1},{17,16},{2,19},{3,2},{18,3},{19,18},{4,21},{5,... | collective-permute-start | bytes 442376 | tf_op jit(solution)/shard_map/ppermute | solution.py:487
  384.7 42.0 %collective-permute-start.29 = (bf16[192,1536]{1,0:T(8,128)(2,1)}, bf16[192,1536]{1,0:T(8,128)(2,1)}, u32[]{:S(2)}, u32[]{:S(2)}) collective-permute-start(bf16[192,1536]{1,0:T(8,128)(2,1)} %get-tuple-element.106), channel_id=1, source_target_pairs={{0,17},{1,0},{16,1},{17,16},{2,19},{3,2},{18,3},{19,18},{4,21},{5,... | collective-permute-start | bytes 1769480 | tf_op jit(solution)/shard_map/ppermute | solution.py:487
  390.4 36.3 %collective-permute-start.30 = (bf16[192,1536]{1,0:T(8,128)(2,1)}, bf16[192,1536]{1,0:T(8,128)(2,1)}, u32[]{:S(2)}, u32[]{:S(2)}) collective-permute-start(bf16[192,1536]{1,0:T(8,128)(2,1)} %get-tuple-element.107), channel_id=1, source_target_pairs={{0,1},{1,16},{16,17},{17,0},{2,3},{3,18},{18,19},{19,2},{4,5},{5,2... | collective-permute-start | bytes 1769480 | tf_op jit(solution)/shard_map/ppermute | solution.py:487
  396.3 30.4 %collective-permute-start.31 = (bf16[192,1536]{1,0:T(8,128)(2,1)}, bf16[192,1536]{1,0:T(8,128)(2,1)}, u32[]{:S(2)}, u32[]{:S(2)}) collective-permute-start(bf16[192,1536]{1,0:T(8,128)(2,1)} %get-tuple-element.108), channel_id=1, source_target_pairs={{0,16},{1,17},{16,0},{17,1},{2,18},{3,19},{18,2},{19,3},{4,20},{5,... | collective-permute-start | bytes 1769480 | tf_op jit(solution)/shard_map/ppermute | solution.py:487
  401.1 19.7 %all-to-all-start.5 = ((bf16[8,12,768]{2,1,0:T(8,128)(2,1)}), bf16[8,12,768]{2,1,0:T(8,128)(2,1)S(1)}, u32[]{:S(2)}, u32[]{:S(2)}) async-start(bf16[8,12,768]{2,1,0:T(8,128)(2,1)} %bitcast_select_fusion), calls=%async_computation.5 | async-start | bytes 393216 | tf_op jit(solution)/shard_map/all_to_all | solution.py:647
  420.8 17.3 %all-to-all-start.7 = ((bf16[16,48,384]{2,1,0:T(8,128)(2,1)}), bf16[16,48,384]{2,1,0:T(8,128)(2,1)S(1)}, u32[]{:S(2)}, u32[]{:S(2)}) async-start(bf16[16,48,384]{2,1,0:T(8,128)(2,1)} %bitcast.85), calls=%async_computation.7 | async-start | bytes 1179648 | tf_op jit(solution)/shard_map/all_to_all | solution.py:606
  (74 other events, 380.8 us)
Sparse Core Ops, SparseCore 0:
  32.5 78.3 all-gather.1
  271.6 84.2 reduce-scatter.3
